TPU v7x, 32 devices: a whole 2x2x4 slice. The times are simulated.
32 devices in a mesh: row: 4 (over y, x), col: 8 (over z, core).
Axes of the slice: x: 2, y: 2, z: 4, core: 2. Of those that a mesh axis runs over, the one named last changes fastest.
Arguments:
- features: bfloat16 [8, 4096, 128], P('col', 'row'), may hold values from 0.099609375 to 3
- relu_mask: int32 [8, 4096, 128], P('col', 'row'), may hold values 0 or 1
- tiles: bfloat16 [4, 8, 184, 256, 256], P('row', 'col'), may hold values from -0.25 to 0.25
- tile_rows: int32 [4, 8, 184], P('row', 'col'), may hold values from 0 to 31, as said below
- tile_cols: int32 [4, 8, 184], P('row', 'col'), may hold values from 0 to 15
- tile_count: int32 [4, 8], P('row', 'col'), may hold values from 23 to 184, as said below
- weight: bfloat16 [128, 128], replicated, may hold values from -0.5 to 0.5
- cotangent: bfloat16 [4, 8192, 128], P('row', 'col'), may hold values from -6 to 6
Outputs:
- out_pre: bfloat16 [4, 8192, 128], P('row', 'col')
- weight_grad: float32 [128, 128], replicated
- input_grad: bfloat16 [8, 4096, 128], P('col', 'row')
Inputs may be any that keep to these rules, and one draw needn't show every extreme that they name: `tile_rows`: within one panel pair the live and dead slots name distinct (block row, block column) pairs. `tile_count`: counts differ widely between panel pairs.
All inputs are finite; a program needn't handle non-finite values. No bound on the sum of `relu_mask` on one device may be relied on, other than what follows from the above.
Results may differ from a plain program's by a relative error of at most 0.022.
Values may be sent and summed in bfloat16 or wider, within the bound.
No kernel may reach another device: no remote copies, remote signals or barrier semaphores. Data moves between devices by JAX's collectives and lax.ppermute only.
A program may use at most 192 MiB of HBM per device.

v0:
```python
import jax
import jax.numpy as jnp
from jax import lax
from jax.sharding import PartitionSpec as P


def slot_products(tile_vals, row_ids, col_ids, source, backward):
    tile_size = tile_vals.shape[1]
    feature_width = source.shape[1]
    if backward:
        blocks = source.reshape(-1, tile_size, feature_width)[row_ids]
        products = jnp.einsum("sij,sif->sjf", tile_vals, blocks, preferred_element_type=jnp.float32)
        target_ids = col_ids
    else:
        blocks = source.reshape(-1, tile_size, feature_width)[col_ids]
        products = jnp.einsum("sij,sjf->sif", tile_vals, blocks, preferred_element_type=jnp.float32)
        target_ids = row_ids
    return (products, target_ids)


def apply_tiles(tile_vals, row_ids, col_ids, live_count, source, backward, segments):
    feature_width = source.shape[1]
    slots = tile_vals.shape[0]
    products, target_ids = slot_products(tile_vals, row_ids, col_ids, source, backward)
    live_slots = jnp.arange(slots, dtype=jnp.int32) < live_count
    targets = jnp.arange(segments, dtype=jnp.int32)[:, None] == target_ids[None, :]
    selector = jnp.where(targets & live_slots[None, :], 1.0, 0.0).astype(jnp.float32)
    total = jnp.einsum(
        "rs,sif->rif",
        selector,
        products,
        precision=lax.Precision.HIGHEST,
        preferred_element_type=jnp.float32,
    )
    return total.reshape(-1, feature_width)


def body(features, relu_mask, tiles, tile_rows, tile_cols, tile_count, weight, cotangent):
    tile_size = tiles.shape[3]
    mask_rows = relu_mask[0]
    hidden = features[0] * mask_rows.astype(jnp.bfloat16)
    tile_vals = tiles[0, 0]
    row_ids = tile_rows[0, 0]
    col_ids = tile_cols[0, 0]
    live_count = tile_count[0, 0]
    own_rows = hidden.shape[0]
    row_blocks = own_rows * lax.axis_size("col") // tile_size
    col_blocks = own_rows * lax.axis_size("row") // tile_size
    feat_panel = lax.all_gather(hidden, "row", axis=0, tiled=True)
    forward_terms = apply_tiles(
        tile_vals, row_ids, col_ids, live_count, feat_panel, False, row_blocks
    )
    forward_terms = lax.optimization_barrier(forward_terms.astype(jnp.bfloat16)).astype(jnp.float32)
    aggregate = lax.psum_scatter(
        forward_terms.astype(jnp.bfloat16), "col", scatter_dimension=0, tiled=True
    )
    out_pre = jnp.dot(aggregate, weight, preferred_element_type=jnp.float32).astype(jnp.bfloat16)
    cot_rows = cotangent[0]
    weight_term = lax.dot_general(
        aggregate, cot_rows, (((0,), (0,)), ((), ())), preferred_element_type=jnp.float32
    )
    grad_scale = 1.0 / jnp.sqrt(jnp.float32(own_rows * lax.axis_size("row") * lax.axis_size("col")))
    weight_grad = lax.psum(weight_term, ("row", "col")) * grad_scale
    grad_rows = lax.dot_general(
        cot_rows, weight, (((1,), (1,)), ((), ())), preferred_element_type=jnp.float32
    )
    grad_rows = lax.all_gather(grad_rows.astype(jnp.bfloat16), "col", axis=0, tiled=True)
    back_terms = apply_tiles(tile_vals, row_ids, col_ids, live_count, grad_rows, True, col_blocks)
    back_terms = lax.optimization_barrier(back_terms.astype(jnp.bfloat16)).astype(jnp.float32)
    summed = lax.psum_scatter(
        back_terms.astype(jnp.bfloat16), "row", scatter_dimension=0, tiled=True
    ).astype(jnp.float32)
    input_grad = (summed * mask_rows.astype(jnp.float32)).astype(jnp.bfloat16)
    return (out_pre[None], weight_grad, input_grad[None])


def solution(mesh):
    placed = (
        P("col", "row", None),
        P("col", "row", None),
        P("row", "col", None, None, None),
        P("row", "col", None),
        P("row", "col", None),
        P("row", "col"),
        P(),
        P("row", "col", None),
    )
    return jax.shard_map(
        body,
        mesh=mesh,
        in_specs=placed,
        out_specs=(P("row", "col", None), P(), P("col", "row", None)),
        check_vma=False,
    )
```

profile of v0, /device:TPU:0, one launch (start us, length us, event | category | flops | bytes accessed | tf_op | source)
XLA Modules:
  0.0 347.6 jit_solution(17806151102796800121)
XLA Ops:
  7.2 0.0 all-gather.6.cloned.1.call-start
  7.2 1.9 convert_multiply_fusion
  9.1 0.0 all-gather.6.cloned.1.call-update
  9.1 0.0 all-gather.4.cloned.1.call-start
  9.2 1.7 convolution_convert_fusion
  10.9 0.0 all-gather.4.cloned.1.call-update
  10.9 0.0 reduce-scatter.3.cloned.1.call-start
  11.6 0.7 compare_select_fusion.1
  12.3 27.5 %all-gather.6.cloned.1.call-done = bf16[1,4096,128]{2,1,0:T(8,128)(2,1)} async-done(((bf16[1,1024,128]{2,1,0:T(8,128)(2,1)}), bf16[1,4096,128]{2,1,0:T(8,128)(2,1)}) %all-gather.6.cloned.1.call-update) | async-done | bytes 1048592 | tf_op jit(solution)/shard_map/all_gather | solution.py:49
  39.8 9.3 %gather_fusion = bf16[184,256,128]{2,1,0:T(8,128)(2,1)} fusion(bf16[16,256,128]{2,1,0:T(8,128)(2,1)} %bitcast.56, s32[1024]{0:T(1024)S(1)} %pad_clamp_fusion.1), kind=kCustom, calls=%fused_computation | custom fusion | bytes 24117984 | tf_op jit(solution)/shard_map/gather | solution.py:15
  49.1 21.4 %fusion.6 = f32[184,128,256]{2,1,0:T(8,128)} fusion(bf16[184,256,128]{2,1,0:T(8,128)(2,1)} %gather_fusion, bf16[1,1,184,256,256]{4,3,2,1,0:T(8,128)(2,1)} %param.10), kind=kOutput, calls=%fused_computation.8 | convolution fusion | flops 3087007744 | bytes 60293120 | tf_op jit(solution)/shard_map/sij,sjf->sif/dot_general | solution.py:16
  70.4 24.5 %copy.13 = f32[184,128,256]{1,0,2:T(8,128)} copy(f32[184,128,256]{2,1,0:T(8,128)} %fusion.6) | data formatting | bytes 48234496 | tf_op jit(solution)/shard_map/sij,sjf->sif/dot_general | solution.py:16
  95.0 17.0 %fusion.8 = bf16[32,256,128]{2,0,1:T(8,128)(2,1)S(1)} fusion(f32[184,128,256]{1,0,2:T(8,128)} %copy.13, s32[184]{0:T(256)S(1)} %bitcast.60, pred[184]{0:T(512)(128)(4,1)S(1)} %iota_compare_fusion.2), kind=kOutput, calls=%fused_computation.10 | convolution fusion | flops 2316322048 | bytes 26215320 | tf_op jit(solution)/shard_map/rs,sif->rif/dot_general | solution.py:28
  111.9 2.1 copy.11
  114.1 0.0 reduce-scatter.3.cloned.1.call-update
  114.1 0.2 reduce-scatter.5.cloned.1.call-start
  114.4 0.0 all-gather.4.cloned.1.call-done
  114.4 9.7 %gather_fusion.1 = bf16[184,256,128]{2,1,0:T(8,128)(2,1)} fusion(bf16[32,256,128]{2,1,0:T(8,128)(2,1)} %bitcast.57, s32[1024]{0:T(1024)S(1)} %pad_clamp_fusion), kind=kCustom, calls=%fused_computation.1 | custom fusion | bytes 24117984 | tf_op jit(solution)/shard_map/gather | solution.py:11
  124.1 22.1 %fusion.4 = f32[184,128,256]{2,1,0:T(8,128)} fusion(bf16[184,256,128]{2,1,0:T(8,128)(2,1)} %gather_fusion.1, bf16[1,1,184,256,256]{4,3,2,1,0:T(8,128)(2,1)} %param.10), kind=kOutput, calls=%fused_computation.6 | convolution fusion | flops 3087007744 | bytes 60293120 | tf_op jit(solution)/shard_map/sij,sif->sjf/dot_general | solution.py:12
  146.2 24.5 %copy.14 = f32[184,128,256]{1,0,2:T(8,128)} copy(f32[184,128,256]{2,1,0:T(8,128)} %fusion.4) | data formatting | bytes 48234496 | tf_op jit(solution)/shard_map/sij,sif->sjf/dot_general | solution.py:12
  170.7 15.1 %fusion.11 = bf16[16,256,128]{2,0,1:T(8,128)(2,1)S(1)} fusion(f32[184,128,256]{1,0,2:T(8,128)} %copy.14, s32[184]{0:T(256)S(1)} %bitcast.61, pred[184]{0:T(512)(128)(4,1)S(1)} %iota_compare_fusion.2), kind=kOutput, calls=%fused_computation.11 | convolution fusion | flops 1158161024 | bytes 25166744 | tf_op jit(solution)/shard_map/rs,sif->rif/dot_general | solution.py:28
  185.8 1.2 copy.12
  187.0 0.0 reduce-scatter.5.cloned.1.call-update
  187.1 0.0 all-reduce.2.cloned.1.call-start
  187.1 0.0 reduce-scatter.3.cloned.1.call-done
  187.1 1.9 fusion.18
  189.0 0.0 all-reduce.2.cloned.1.call-update
  189.0 1.9 fusion.14
  190.9 24.2 %reduce-scatter.5.cloned.1.call-done = bf16[1024,128]{1,0:T(8,128)(2,1)} async-done(((bf16[4096,128]{1,0:T(8,128)(2,1)}), bf16[1024,128]{1,0:T(8,128)(2,1)}) %reduce-scatter.5.cloned.1.call-update) | async-done | bytes 262160 | tf_op jit(solution)/shard_map/reduce_scatter | solution.py:70
  215.1 1.7 fusion.16
  216.8 122.8 %all-reduce.2.cloned.1.call-done = f32[128,128]{1,0:T(8,128)} async-done(((f32[128,128]{1,0:T(8,128)}), f32[128,128]{1,0:T(8,128)}) %all-reduce.2.cloned.1.call-update) | async-done | bytes 65552 | tf_op jit(solution)/shard_map/psum | solution.py:63
  339.6 1.5 broadcast_multiply_fusion
  (14 shorter events, 0.0 us)
Async XLA Ops:
  7.2 2.0 copy-start
  7.2 32.6 %all-gather.6.cloned.1.call-start = ((), (), s32[]{:S(2)}) async-start(), calls=%async_computation.6 | async-start | bytes 1310720 | tf_op jit(solution)/shard_map/all_gather | solution.py:49
  9.1 105.2 %all-gather.4.cloned.1.call-start = ((), (), s32[]{:S(2)}) async-start(), calls=%async_computation.4 | async-start | bytes 2359296 | tf_op jit(solution)/shard_map/all_gather | solution.py:67
  10.9 176.2 %reduce-scatter.3.cloned.1.call-start = ((), (), s32[]{:S(2)}) async-start(), calls=%async_computation.2 | async-start | bytes 2359296 | tf_op jit(solution)/shard_map/reduce_scatter | solution.py:54
  70.4 24.5 %copy-start.3 = (s32[1,1,184]{2,1,0:T(1,128)S(1)}, s32[1,1,184]{2,1,0:T(1,128)}, u32[]{:S(2)}) copy-start(s32[1,1,184]{2,1,0:T(1,128)} %param.11) | copy-start | bytes 2212
  114.1 101.0 %reduce-scatter.5.cloned.1.call-start = ((), (), s32[]{:S(2)}) async-start(), calls=%async_computation.5 | async-start | bytes 1310720 | tf_op jit(solution)/shard_map/reduce_scatter | solution.py:70
  146.2 24.5 %copy-start.4 = (s32[1,1,184]{2,1,0:T(1,128)S(1)}, s32[1,1,184]{2,1,0:T(1,128)}, u32[]{:S(2)}) copy-start(s32[1,1,184]{2,1,0:T(1,128)} %param.12) | copy-start | bytes 2212
  170.7 18.3 %copy-start.2 = (bf16[128,128]{1,0:T(8,128)(2,1)S(1)}, bf16[128,128]{1,0:T(8,128)(2,1)}, u32[]{:S(2)}) copy-start(bf16[128,128]{1,0:T(8,128)(2,1)} %param.14) | copy-start | bytes 98308
  170.7 44.4 %copy-start.1 = (s32[1,1024,128]{2,1,0:T(8,128)S(1)}, s32[1,1024,128]{2,1,0:T(8,128)}, u32[]{:S(2)}) copy-start(s32[1,1024,128]{2,1,0:T(8,128)} %param.9) | copy-start | bytes 1572868
  187.1 152.5 %all-reduce.2.cloned.1.call-start = ((), (), s32[]{:S(2)}) async-start(), calls=%async_computation.3 | async-start | bytes 131072 | tf_op jit(solution)/shard_map/psum | solution.py:63
Sparse Core Ops, SparseCore 0:
  10.4 29.3 all-gather.5
  42.0 29.0 all-gather.3
  114.2 35.9 reduce-scatter.2
  187.2 27.8 reduce-scatter.4
  222.0 117.5 all-reduce.1
where the time goes:
time: 350 us; the launch traced here: 348 us
  waiting for transfers between devices  175 us (50%)
  matrix products  81 us (23%)
  local copies, waits for them, and re-layouts  71.4 us (20%)
  between operations  14.5 us (4%)
  other arithmetic  5.8 us (2%)
    psum x1, waiting for transfers between devices, body(): weight_grad = lax.psum(weight_term, ('row', 'col')) * grad_scale  123 us
    dot_general x2, matrix products, apply_tiles(): jnp.einsum('rs,sif->rif', selector, products, precision=lax.Precision.HIG...  32.1 us
    all_gather x1, waiting for transfers between devices, body(): feat_panel = lax.all_gather(hidden, 'row', axis=0, tiled=True)  27.5 us
    dot_general x1, local copies, waits for them, and re-layouts, slot_products(): jnp.einsum('sij,sif->sjf', tile_vals, blocks, preferred_element_type=jnp....  24.5 us
    dot_general x1, local copies, waits for them, and re-layouts, slot_products(): jnp.einsum('sij,sjf->sif', tile_vals, blocks, preferred_element_type=jnp....  24.5 us
    reduce_scatter x1, waiting for transfers between devices, body(): lax.psum_scatter(back_terms.astype(jnp.bfloat16), 'row', scatter_dimensio...  24.2 us
    dot_general x1, matrix products, slot_products(): jnp.einsum('sij,sif->sjf', tile_vals, blocks, preferred_element_type=jnp....  22.1 us
    dot_general x1, matrix products, slot_products(): jnp.einsum('sij,sjf->sif', tile_vals, blocks, preferred_element_type=jnp....  21.4 us
  transfers between devices with their start and end apart: 5, of which 3 were waited for; matrix products, arithmetic and copies ran while one was open for 45% of the time, Pallas kernels for 0%

commit v1 on v0

v1 whole, which is shorter than its diff:
```python
import functools
import math

import jax
import jax.numpy as jnp
from jax import lax
from jax.experimental import pallas as pl
from jax.experimental.pallas import tpu as pltpu
from jax.sharding import PartitionSpec as P

CORES = 2
VMEM_LIMIT = 50 * 2**20
F32 = jnp.float32
BF16 = jnp.bfloat16
ANY = pl.BlockSpec(memory_space=pl.ANY)
SMEM = pl.BlockSpec(memory_space=pltpu.SMEM)
VMEM = pl.BlockSpec(memory_space=pltpu.VMEM)
PARAMS = pltpu.CompilerParams(vmem_limit_bytes=VMEM_LIMIT)


def swap(value, axis, step):
    size = lax.axis_size(axis)
    return lax.ppermute(value, axis, [(i, i ^ step) for i in range(size)])


def chunk_of(slots):
    return math.gcd(slots, 8)


def tile_copies(tiles, buf, sems):
    chunk = chunk_of(buf.shape[0])

    def copy(i):
        span = pl.ds(i * chunk, chunk)
        return pltpu.make_async_copy(tiles.at[0, 0, span], buf.at[span], sems.at[i])

    return copy


def forward_kernel(n_shards, count_ref, rows_ref, cols_ref, tiles, *refs):
    shards, (keep, send) = refs[:n_shards], refs[n_shards : n_shards + 2]
    buf, panel, acc, tile_sems, panel_sems = refs[n_shards + 2 :]
    slots, tile = buf.shape[:2]
    own = shards[0].shape[0]
    chunk = chunk_of(slots)
    dump = acc.shape[0] - 1
    live = count_ref[0, 0]
    chunks = pl.cdiv(live, chunk)
    row, col = lax.axis_index("row"), lax.axis_index("col")
    line, core = col // CORES, col % CORES
    copy = tile_copies(tiles, buf, tile_sems)

    def panel_copy(k):
        place = pl.multiple_of((row ^ k) * own, own)
        return pltpu.make_async_copy(shards[k], panel.at[pl.ds(place, own)], panel_sems.at[k])

    for k in range(n_shards):
        panel_copy(k).start()

    @pl.loop(0, chunks)
    def _(i):
        copy(i).start()

    acc[...] = jnp.zeros_like(acc)
    for k in range(n_shards):
        panel_copy(k).wait()

    @pl.loop(0, chunks)
    def _(i):
        copy(i).wait()
        for j in range(chunk):
            s = i * chunk + j
            c = cols_ref[0, 0, s]
            r = jnp.where(s < live, rows_ref[0, 0, s], dump)
            source = panel[pl.ds(pl.multiple_of(c * tile, tile), tile), :]
            acc[r] += jnp.dot(buf[s], source, preferred_element_type=F32)

    per = own // tile
    for k in range(keep.shape[0] // own):
        base = (line ^ k) * CORES
        for b in range(per):
            span = pl.ds(k * own + b * tile, tile)
            keep[span, :] = acc[(base + core) * per + b].astype(BF16)
            send[span, :] = acc[(base + 1 - core) * per + b].astype(BF16)


def backward_kernel(n_rows, n_lines, count_ref, rows_ref, cols_ref, tiles, scale, *refs):
    n_cots = n_lines * CORES
    hids, cots, refs = refs[:n_rows], refs[n_rows : n_rows + n_cots], refs[n_rows + n_cots :]
    outs, weight_term, refs = refs[:n_rows], refs[n_rows], refs[n_rows + 1 :]
    buf, panel, turned, hidden, acc, tile_sems, panel_sems = refs
    slots, tile = buf.shape[:2]
    own = hids[0].shape[0]
    per = own // tile
    chunk = chunk_of(slots)
    dump = acc.shape[0] - 1
    live = count_ref[0, 0]
    chunks = pl.cdiv(live, chunk)
    row, col = lax.axis_index("row"), lax.axis_index("col")
    line, core = col // CORES, col % CORES
    copy = tile_copies(tiles, buf, tile_sems)

    def cot_copy(k):
        place = ((line ^ (k // CORES)) * CORES + (core ^ (k % CORES))) * own
        span = pl.ds(pl.multiple_of(place, own), own)
        return pltpu.make_async_copy(cots[k], panel.at[span], panel_sems.at[k])

    def hid_copy(k):
        span = pl.ds(pl.multiple_of((row ^ k) * own, own), own)
        return pltpu.make_async_copy(hids[k], hidden.at[span], panel_sems.at[n_cots + k])

    for k in range(n_cots):
        cot_copy(k).start()

    @pl.loop(0, chunks)
    def _(i):
        copy(i).start()

    for k in range(n_rows):
        hid_copy(k).start()
    acc[...] = jnp.zeros_like(acc)
    for k in range(n_cots):
        cot_copy(k).wait()
    for b in range(turned.shape[0]):
        turned[b] = panel[b * tile : (b + 1) * tile, :].T

    @pl.loop(0, chunks)
    def _(i):
        copy(i).wait()
        for j in range(chunk):
            s = i * chunk + j
            r = rows_ref[0, 0, s]
            c = jnp.where(s < live, cols_ref[0, 0, s], dump)
            acc[c] += jnp.dot(turned[r], buf[s], preferred_element_type=F32)

    for k in range(n_rows):
        hid_copy(k).wait()
    total = jnp.zeros(weight_term.shape, F32)
    for b in range(acc.shape[0] - 1):
        total += jnp.dot(
            acc[b].astype(BF16), hidden[b * tile : (b + 1) * tile, :], preferred_element_type=F32
        )
    weight_term[...] = total.T * scale[0]
    for k in range(n_rows):
        for b in range(per):
            outs[k][b * tile : (b + 1) * tile, :] = acc[(row ^ k) * per + b].T.astype(BF16)


def pair_kernel(keep, got, *outs):
    own = outs[0].shape[0]
    for k, out in enumerate(outs):
        span = pl.ds(k * own, own)
        out[...] = (keep[span, :].astype(F32) + got[span, :].astype(F32)).astype(BF16)


def summed(parts):
    total = parts[0][...].astype(F32)
    for part in parts[1:]:
        total += part[...].astype(F32)
    return total.astype(BF16)


def out_kernel(weight, *refs):
    refs[-1][0] = jnp.dot(summed(refs[:-1]), weight[...], preferred_element_type=F32).astype(BF16)


def grad_kernel(weight, mask, *refs):
    turned = lax.dot_general(
        summed(refs[:-1]), weight[...], (((1,), (1,)), ((), ())), preferred_element_type=F32
    )
    refs[-1][0] = (turned * mask[0].astype(F32)).astype(BF16)


def body(features, relu_mask, tiles, tile_rows, tile_cols, tile_count, weight, cotangent):
    slots, tile = tiles.shape[2:4]
    own, width = features.shape[1:]
    n_rows, n_cols = lax.axis_size("row"), lax.axis_size("col")
    n_lines = n_cols // CORES
    row_blocks, col_blocks = own * n_cols // tile, own * n_rows // tile
    ids = (tile_count, tile_rows, tile_cols, tiles)
    block = jax.ShapeDtypeStruct((own, width), BF16)

    cot = cotangent[0]
    cots = [cot] + [swap(cot, "col", CORES * k) for k in range(1, n_lines)]
    cots = [part for mine in cots for part in (mine, swap(mine, "col", 1))]
    hidden = features[0] * relu_mask[0].astype(BF16)
    hids = [hidden] + [swap(hidden, "row", k) for k in range(1, n_rows)]

    half = jax.ShapeDtypeStruct((n_lines * own, width), BF16)
    keep, send = pl.pallas_call(
        functools.partial(forward_kernel, n_rows),
        out_shape=(half, half),
        in_specs=[SMEM] * 3 + [ANY] * (1 + n_rows),
        out_specs=(VMEM, VMEM),
        scratch_shapes=[
            pltpu.VMEM((slots, tile, tile), BF16),
            pltpu.VMEM((n_rows * own, width), BF16),
            pltpu.VMEM((row_blocks + 1, tile, width), F32),
            pltpu.SemaphoreType.DMA((slots // chunk_of(slots),)),
            pltpu.SemaphoreType.DMA((n_rows,)),
        ],
        compiler_params=PARAMS,
        name="forward_tiles",
    )(*ids, *hids)
    got = swap(send, "col", 1)
    pairs = pl.pallas_call(
        pair_kernel,
        out_shape=(block,) * n_lines,
        in_specs=[VMEM] * 2,
        out_specs=(VMEM,) * n_lines,
        name="pair_sum",
    )(keep, got)
    parts = [pairs[0]] + [swap(pairs[k], "col", CORES * k) for k in range(1, n_lines)]
    out_pre = pl.pallas_call(
        out_kernel,
        out_shape=jax.ShapeDtypeStruct((1, own, width), BF16),
        in_specs=[VMEM] * (1 + n_lines),
        out_specs=VMEM,
        name="out_pre",
    )(weight, *parts)

    scale = 1.0 / jnp.sqrt(jnp.full((1,), own * n_rows * n_cols, F32))
    *backs, weight_term = pl.pallas_call(
        functools.partial(backward_kernel, n_rows, n_lines),
        out_shape=(block,) * n_rows + (jax.ShapeDtypeStruct((width, width), F32),),
        in_specs=[SMEM] * 3 + [ANY] + [SMEM] + [ANY] * (n_rows + n_cols),
        out_specs=(VMEM,) * (n_rows + 1),
        scratch_shapes=[
            pltpu.VMEM((slots, tile, tile), BF16),
            pltpu.VMEM((n_cols * own, width), BF16),
            pltpu.VMEM((row_blocks, width, tile), BF16),
            pltpu.VMEM((n_rows * own, width), BF16),
            pltpu.VMEM((col_blocks + 1, width, tile), F32),
            pltpu.SemaphoreType.DMA((slots // chunk_of(slots),)),
            pltpu.SemaphoreType.DMA((n_cols + n_rows,)),
        ],
        compiler_params=PARAMS,
        name="backward_tiles",
    )(*ids, scale, *hids, *cots)
    backs = [backs[0]] + [swap(backs[k], "row", k) for k in range(1, n_rows)]
    input_grad = pl.pallas_call(
        grad_kernel,
        out_shape=jax.ShapeDtypeStruct((1, own, width), BF16),
        in_specs=[VMEM] * (2 + n_rows),
        out_specs=VMEM,
        name="input_grad",
    )(weight, relu_mask, *backs)

    for axis, size in (("col", n_cols), ("row", n_rows)):
        for bit in range(size.bit_length() - 1):
            weight_term = weight_term + swap(weight_term, axis, 1 << bit)
    return (out_pre, weight_term, input_grad)


def solution(mesh):
    placed = (
        P("col", "row", None),
        P("col", "row", None),
        P("row", "col", None, None, None),
        P("row", "col", None),
        P("row", "col", None),
        P("row", "col"),
        P(),
        P("row", "col", None),
    )
    return jax.shard_map(
        body,
        mesh=mesh,
        in_specs=placed,
        out_specs=(P("row", "col", None), P(), P("col", "row", None)),
        check_vma=False,
    )
```

time: 350 us -> 115 us (0.33)
  the two profiles are of different devices: /device:TPU:0 before, /device:TPU:8 now
where the time goes in v1:
time: 115 us; the launch traced here: 114 us
  waiting for transfers between devices  54.5 us (47%)
  starting transfers between devices  29.7 us (26%)
  Pallas kernels  21.6 us (19%)
  local copies, waits for them, and re-layouts  5.37 us (5%)
  other arithmetic  1.88 us (2%)
  between operations  1.4 us (1%)
    ppermute x22, waiting for transfers between devices, swap(): return lax.ppermute(value, axis, [(i, i ^ step) for i in range(size)])  54.5 us
    ppermute x22, starting transfers between devices, swap(): return lax.ppermute(value, axis, [(i, i ^ step) for i in range(size)])  29.7 us
    pallas_call x1, Pallas kernels, body(): pl.pallas_call(functools.partial(forward_kernel, n_rows), out_shape=(half...  7.6 us
    pallas_call x1, Pallas kernels, body(): pl.pallas_call(functools.partial(backward_kernel, n_rows, n_lines), out_s...  6.96 us
    unnamed x26, local copies, waits for them, and re-layouts  5.37 us
    pallas_call x1, Pallas kernels, body(): pl.pallas_call(pair_kernel, out_shape=(block,) * n_lines, in_specs=[VMEM]...  2.57 us
    pallas_call x1, Pallas kernels, body(): pl.pallas_call(grad_kernel, out_shape=jax.ShapeDtypeStruct((1, own, width...  2.33 us
  transfers between devices with their start and end apart: 22, of which 13 were waited for; matrix products, arithmetic and copies ran while one was open for 1% of the time, Pallas kernels for 10%

profile of v1, /device:TPU:8, one launch (start us, length us, event | category | flops | bytes accessed | tf_op | source)
XLA Modules:
  0.0 114.5 jit_solution(6933740136665900755)
XLA Ops:
  0.6 1.2 %multiply_bitcast_fusion.refs_0_ = bf16[1024,128]{1,0:T(8,128)(2,1)S(1)} fusion(bf16[1,1024,128]{2,1,0:T(8,128)(2,1)} %param.8, s32[1,1024,128]{2,1,0:T(8,128)} %mask.1), kind=kLoop, calls=%fused_computation | loop fusion | flops 262144 | bytes 1048576 | tf_op jit(solution)/shard_map/mul | solution.py:186
  1.8 2.5 %collective-permute-start.2 = (bf16[1024,128]{1,0:T(8,128)(2,1)S(1)}, bf16[1024,128]{1,0:T(8,128)(2,1)S(1)}, u32[]{:S(2)}, u32[]{:S(2)}) collective-permute-start(bf16[1024,128]{1,0:T(8,128)(2,1)S(1)} %multiply_bitcast_fusion.refs_0_), channel_id=1, source_target_pairs={{0,24},{8,16},{16,8},{24,0},{1,25},{9,17},{17,9},{25,1},{2,26},{10... | collective-permute-start | bytes 786440 | tf_op jit(solution)/shard_map/ppermute | solution.py:23
  6.1 6.0 %collective-permute-done.2.refs_3_ = bf16[1024,128]{1,0:T(8,128)(2,1)S(1)} collective-permute-done((bf16[1024,128]{1,0:T(8,128)(2,1)S(1)}, bf16[1024,128]{1,0:T(8,128)(2,1)S(1)}, u32[]{:S(2)}, u32[]{:S(2)}) %collective-permute-start.2) | collective-permute-done | bytes 262176 | tf_op jit(solution)/shard_map/ppermute | solution.py:23
  12.0 4.4 %collective-permute-done.1.refs_2_ = bf16[1024,128]{1,0:T(8,128)(2,1)S(1)} collective-permute-done((bf16[1024,128]{1,0:T(8,128)(2,1)S(1)}, bf16[1024,128]{1,0:T(8,128)(2,1)S(1)}, u32[]{:S(2)}, u32[]{:S(2)}) %collective-permute-start.1) | collective-permute-done | bytes 262176 | tf_op jit(solution)/shard_map/ppermute | solution.py:23
  17.9 7.6 %forward_tiles.1 = (bf16[4096,128]{1,0:T(8,128)(2,1)S(1)}, bf16[4096,128]{1,0:T(8,128)(2,1)S(1)}) custom-call(s32[1,1]{1,0:T(1,128)S(6)} %copy.11.count_ref, s32[1,1,184]{2,1,0:T(1,128)S(1)} %copy-done.3, s32[1,1,184]{2,1,0:T(1,128)S(1)} %copy-done.4, bf16[1,1,184,256,256]{4,3,2,1,0:T(8,128)(2,1)} %tiles.3, ...), custom_call_target="tpu_custom_call" | custom-call | tf_op jit(solution)/shard_map/forward_tiles/pallas_call | solution.py:190
  25.5 1.0 copy-done
  26.5 4.8 %collective-permute-start.3 = (bf16[4096,128]{1,0:T(8,128)(2,1)S(1)}, bf16[4096,128]{1,0:T(8,128)(2,1)S(1)}, u32[]{:S(2)}, u32[]{:S(2)}) collective-permute-start(bf16[4096,128]{1,0:T(8,128)(2,1)S(1)} %get-tuple-element.15), channel_id=1, source_target_pairs={{0,1},{1,0},{2,3},{3,2},{4,5},{5,4},{6,7},{7,6},{8,9},{9,8},{10,11... | collective-permute-start | bytes 3145736 | tf_op jit(solution)/shard_map/ppermute | solution.py:23
  31.3 2.6 %collective-permute-start.10 = (bf16[1024,128]{1,0:T(8,128)(2,1)S(1)}, bf16[1024,128]{1,0:T(8,128)(2,1)S(1)}, u32[]{:S(2)}, u32[]{:S(2)}) collective-permute-start(bf16[1024,128]{1,0:T(8,128)(2,1)S(1)} %bitcast.4), channel_id=1, source_target_pairs={{0,4},{1,5},{2,6},{3,7},{4,0},{5,1},{6,2},{7,3},{8,12},{9,13},{10,... | collective-permute-start | bytes 786440 | tf_op jit(solution)/shard_map/ppermute | solution.py:23
  33.9 1.4 %collective-permute-start.8 = (bf16[1024,128]{1,0:T(8,128)(2,1)S(1)}, bf16[1024,128]{1,0:T(8,128)(2,1)S(1)}, u32[]{:S(2)}, u32[]{:S(2)}) collective-permute-start(bf16[1024,128]{1,0:T(8,128)(2,1)S(1)} %bitcast.5), channel_id=1, source_target_pairs={{0,2},{1,3},{2,0},{3,1},{4,6},{5,7},{6,4},{7,5},{8,10},{9,11},{10,... | collective-permute-start | bytes 786440 | tf_op jit(solution)/shard_map/ppermute | solution.py:23
  35.3 16.3 %collective-permute-done.12.refs_10_ = bf16[1024,128]{1,0:T(8,128)(2,1)S(1)} collective-permute-done((bf16[1024,128]{1,0:T(8,128)(2,1)S(1)}, bf16[1024,128]{1,0:T(8,128)(2,1)S(1)}, u32[]{:S(2)}, u32[]{:S(2)}) %collective-permute-start.12) | collective-permute-done | bytes 262176 | tf_op jit(solution)/shard_map/ppermute | solution.py:23
  51.7 2.5 %collective-permute-done.10.refs_8_ = bf16[1024,128]{1,0:T(8,128)(2,1)S(1)} collective-permute-done((bf16[1024,128]{1,0:T(8,128)(2,1)S(1)}, bf16[1024,128]{1,0:T(8,128)(2,1)S(1)}, u32[]{:S(2)}, u32[]{:S(2)}) %collective-permute-start.10) | collective-permute-done | bytes 262176 | tf_op jit(solution)/shard_map/ppermute | solution.py:23
  54.7 1.0 collective-permute-done.11.refs_9_
  56.0 7.0 %backward_tiles.1 = (bf16[1024,128]{1,0:T(8,128)(2,1)S(1)}, bf16[1024,128]{1,0:T(8,128)(2,1)S(1)}, bf16[1024,128]{1,0:T(8,128)(2,1)S(1)}, bf16[1024,128]{1,0:T(8,128)(2,1)S(1)}, f32[128,128]{1,0:T(8,128)S(1)}) custom-call(s32[1,1]{1,0:T(1,128)S(6)} %copy.11.count_ref, s32[1,1,184]{2,1,0:T(1,128)S(1)} %copy-done.3, s32[1,1,184]{2,1,0:T(1,128)S(1)} %copy-done.4, ...), custom_call_target="tpu_custom_call" | custom-call | tf_op jit(solution)/shard_map/backward_tiles/pallas_call | solution.py:223
  63.7 3.7 %collective-permute-start.14 = (f32[128,128]{1,0:T(8,128)S(1)}, f32[128,128]{1,0:T(8,128)S(1)}, u32[]{:S(2)}, u32[]{:S(2)}) collective-permute-start(f32[128,128]{1,0:T(8,128)S(1)} %get-tuple-element.20), channel_id=1, source_target_pairs={{0,1},{1,0},{2,3},{3,2},{4,5},{5,4},{6,7},{7,6},{8,9},{9,8},{10,11... | collective-permute-start | bytes 196616 | tf_op jit(solution)/shard_map/ppermute | solution.py:23
  68.3 3.7 %collective-permute-start.15 = (f32[128,128]{1,0:T(8,128)S(1)}, f32[128,128]{1,0:T(8,128)S(1)}, u32[]{:S(2)}, u32[]{:S(2)}) collective-permute-start(f32[128,128]{1,0:T(8,128)S(1)} %add.15), channel_id=1, source_target_pairs={{0,2},{1,3},{2,0},{3,1},{4,6},{5,7},{6,4},{7,5},{8,10},{9,11},{10,... | collective-permute-start | bytes 196616 | tf_op jit(solution)/shard_map/ppermute | solution.py:23
  72.0 2.6 %collective-permute-done.15 = f32[128,128]{1,0:T(8,128)S(1)} collective-permute-done((f32[128,128]{1,0:T(8,128)S(1)}, f32[128,128]{1,0:T(8,128)S(1)}, u32[]{:S(2)}, u32[]{:S(2)}) %collective-permute-start.15) | collective-permute-done | bytes 65568 | tf_op jit(solution)/shard_map/ppermute | solution.py:23
  74.6 1.5 %collective-permute-start.16 = (f32[128,128]{1,0:T(8,128)S(1)}, f32[128,128]{1,0:T(8,128)S(1)}, u32[]{:S(2)}, u32[]{:S(2)}) collective-permute-start(f32[128,128]{1,0:T(8,128)S(1)} %add.16), channel_id=1, source_target_pairs={{0,4},{1,5},{2,6},{3,7},{4,0},{5,1},{6,2},{7,3},{8,12},{9,13},{10,... | collective-permute-start | bytes 196616 | tf_op jit(solution)/shard_map/ppermute | solution.py:23
  76.2 3.7 %collective-permute-done.16 = f32[128,128]{1,0:T(8,128)S(1)} collective-permute-done((f32[128,128]{1,0:T(8,128)S(1)}, f32[128,128]{1,0:T(8,128)S(1)}, u32[]{:S(2)}, u32[]{:S(2)}) %collective-permute-start.16) | collective-permute-done | bytes 65568 | tf_op jit(solution)/shard_map/ppermute | solution.py:23
  79.9 0.8 collective-permute-start.17
  80.7 1.6 %collective-permute-start.21 = (bf16[1024,128]{1,0:T(8,128)(2,1)S(1)}, bf16[1024,128]{1,0:T(8,128)(2,1)S(1)}, u32[]{:S(2)}, u32[]{:S(2)}) collective-permute-start(bf16[1024,128]{1,0:T(8,128)(2,1)S(1)} %get-tuple-element.24), channel_id=1, source_target_pairs={{0,24},{8,16},{16,8},{24,0},{1,25},{9,17},{17,9},{25,1},{2,26},{10... | collective-permute-start | bytes 786440 | tf_op jit(solution)/shard_map/ppermute | solution.py:23
  82.3 1.0 copy-done.5
  83.2 2.6 %pair_sum.1 = (bf16[1024,128]{1,0:T(8,128)(2,1)}, bf16[1024,128]{1,0:T(8,128)(2,1)}, bf16[1024,128]{1,0:T(8,128)(2,1)}, bf16[1024,128]{1,0:T(8,128)(2,1)}) custom-call(bf16[4096,128]{1,0:T(8,128)(2,1)} %copy-done, bf16[4096,128]{1,0:T(8,128)(2,1)} %copy-done.5), custom_call_target="tpu_custom_call" | custom-call | tf_op jit(solution)/shard_map/pair_sum/pallas_call | solution.py:206
  85.8 2.2 %collective-permute-start.4 = (bf16[1024,128]{1,0:T(8,128)(2,1)}, bf16[1024,128]{1,0:T(8,128)(2,1)S(1)}, u32[]{:S(2)}, u32[]{:S(2)}) collective-permute-start(bf16[1024,128]{1,0:T(8,128)(2,1)} %get-tuple-element.17), channel_id=1, source_target_pairs={{0,2},{1,3},{2,0},{3,1},{4,6},{5,7},{6,4},{7,5},{8,10},{9,11},{10,... | collective-permute-start | bytes 786440 | tf_op jit(solution)/shard_map/ppermute | solution.py:23
  88.0 1.5 %collective-permute-start.6 = (bf16[1024,128]{1,0:T(8,128)(2,1)}, bf16[1024,128]{1,0:T(8,128)(2,1)S(1)}, u32[]{:S(2)}, u32[]{:S(2)}) collective-permute-start(bf16[1024,128]{1,0:T(8,128)(2,1)} %get-tuple-element.19), channel_id=1, source_target_pairs={{0,6},{1,7},{2,4},{3,5},{4,2},{5,3},{6,0},{7,1},{8,14},{9,15},{10,... | collective-permute-start | bytes 786440 | tf_op jit(solution)/shard_map/ppermute | solution.py:23
  89.5 1.4 %collective-permute-start.18 = (f32[128,128]{1,0:T(8,128)S(1)}, f32[128,128]{1,0:T(8,128)S(1)}, u32[]{:S(2)}, u32[]{:S(2)}) collective-permute-start(f32[128,128]{1,0:T(8,128)S(1)} %add.18), channel_id=1, source_target_pairs={{0,16},{8,24},{16,0},{24,8},{1,17},{9,25},{17,1},{25,9},{2,18},{10... | collective-permute-start | bytes 196616 | tf_op jit(solution)/shard_map/ppermute | solution.py:23
  91.0 0.7 copy-done.9
  91.7 2.3 %input_grad.1 = bf16[1,1024,128]{2,1,0:T(8,128)(2,1)} custom-call(bf16[128,128]{1,0:T(8,128)(2,1)} %weight.3, s32[1,1024,128]{2,1,0:T(8,128)} %mask.1, bf16[1024,128]{1,0:T(8,128)(2,1)} %copy-done.2, bf16[1024,128]{1,0:T(8,128)(2,1)} %copy-done.7, bf16[1024,128]{1,0:T(8,128)(2,1)} %copy-done.8, bf16[1024,128]{1,0:T(8,128)(2,1)} %copy-done.9), custom_call_target="tpu_custom_call" | custom-call | tf_op jit(solution)/shard_map/input_grad/pallas_call | solution.py:241
  94.7 2.5 %collective-permute-done.4.refs_1_ = bf16[1024,128]{1,0:T(8,128)(2,1)S(1)} collective-permute-done((bf16[1024,128]{1,0:T(8,128)(2,1)}, bf16[1024,128]{1,0:T(8,128)(2,1)S(1)}, u32[]{:S(2)}, u32[]{:S(2)}) %collective-permute-start.4) | collective-permute-done | bytes 262176 | tf_op jit(solution)/shard_map/ppermute | solution.py:23
  97.2 9.1 %collective-permute-done.5.refs_2_ = bf16[1024,128]{1,0:T(8,128)(2,1)S(1)} collective-permute-done((bf16[1024,128]{1,0:T(8,128)(2,1)}, bf16[1024,128]{1,0:T(8,128)(2,1)S(1)}, u32[]{:S(2)}, u32[]{:S(2)}) %collective-permute-start.5) | collective-permute-done | bytes 262176 | tf_op jit(solution)/shard_map/ppermute | solution.py:23
  106.3 5.3 %collective-permute-done.6.refs_3_ = bf16[1024,128]{1,0:T(8,128)(2,1)S(1)} collective-permute-done((bf16[1024,128]{1,0:T(8,128)(2,1)}, bf16[1024,128]{1,0:T(8,128)(2,1)S(1)}, u32[]{:S(2)}, u32[]{:S(2)}) %collective-permute-start.6) | collective-permute-done | bytes 262176 | tf_op jit(solution)/shard_map/ppermute | solution.py:23
  111.6 0.7 copy-done.12
  112.3 2.2 %out_pre.1 = bf16[1,1024,128]{2,1,0:T(8,128)(2,1)} custom-call(bf16[128,128]{1,0:T(8,128)(2,1)} %weight.3, bf16[1024,128]{1,0:T(8,128)(2,1)} %get-tuple-element.16.refs_0_, bf16[1024,128]{1,0:T(8,128)(2,1)} %copy-done.10, bf16[1024,128]{1,0:T(8,128)(2,1)} %copy-done.11, bf16[1024,128]{1,0:T(8,128)(2,1)} %copy-done.12), custom_call_target="tpu_custom_call" | custom-call | tf_op jit(solution)/shard_map/out_pre/pallas_call | solution.py:214
  (49 shorter events, 5.7 us)
Async XLA Ops:
  0.6 30.6 %copy-start.1 = (bf16[1,1024,128]{2,1,0:T(8,128)(2,1)S(1)}, bf16[1,1024,128]{2,1,0:T(8,128)(2,1)}, u32[]{:S(2)}) copy-start(bf16[1,1024,128]{2,1,0:T(8,128)(2,1)} %param.15) | copy-start | bytes 786436
  1.8 10.2 %collective-permute-start.2 = (bf16[1024,128]{1,0:T(8,128)(2,1)S(1)}, bf16[1024,128]{1,0:T(8,128)(2,1)S(1)}, u32[]{:S(2)}, u32[]{:S(2)}) collective-permute-start(bf16[1024,128]{1,0:T(8,128)(2,1)S(1)} %multiply_bitcast_fusion.refs_0_), channel_id=1, source_target_pairs={{0,24},{8,16},{16,8},{24,0},{1,25},{9,17},{17,9},{25,1},{2,26},{10... | collective-permute-start | bytes 786440 | tf_op jit(solution)/shard_map/ppermute | solution.py:23
  4.4 12.1 %collective-permute-start.1 = (bf16[1024,128]{1,0:T(8,128)(2,1)S(1)}, bf16[1024,128]{1,0:T(8,128)(2,1)S(1)}, u32[]{:S(2)}, u32[]{:S(2)}) collective-permute-start(bf16[1024,128]{1,0:T(8,128)(2,1)S(1)} %multiply_bitcast_fusion.refs_0_), channel_id=1, source_target_pairs={{0,16},{8,24},{16,0},{24,8},{1,17},{9,25},{17,1},{25,9},{2,18},{10... | collective-permute-start | bytes 786440 | tf_op jit(solution)/shard_map/ppermute | solution.py:23
  4.9 11.7 %collective-permute-start = (bf16[1024,128]{1,0:T(8,128)(2,1)S(1)}, bf16[1024,128]{1,0:T(8,128)(2,1)S(1)}, u32[]{:S(2)}, u32[]{:S(2)}) collective-permute-start(bf16[1024,128]{1,0:T(8,128)(2,1)S(1)} %multiply_bitcast_fusion.refs_0_), channel_id=1, source_target_pairs={{0,8},{8,0},{16,24},{24,16},{1,9},{9,1},{17,25},{25,17},{2,10},{10... | collective-permute-start | bytes 786440 | tf_op jit(solution)/shard_map/ppermute | solution.py:23
  25.5 1.0 copy-start
  26.5 55.8 %collective-permute-start.3 = (bf16[4096,128]{1,0:T(8,128)(2,1)S(1)}, bf16[4096,128]{1,0:T(8,128)(2,1)S(1)}, u32[]{:S(2)}, u32[]{:S(2)}) collective-permute-start(bf16[4096,128]{1,0:T(8,128)(2,1)S(1)} %get-tuple-element.15), channel_id=1, source_target_pairs={{0,1},{1,0},{2,3},{3,2},{4,5},{5,4},{6,7},{7,6},{8,9},{9,8},{10,11... | collective-permute-start | bytes 3145736 | tf_op jit(solution)/shard_map/ppermute | solution.py:23
  31.3 20.4 %collective-permute-start.12 = (bf16[1024,128]{1,0:T(8,128)(2,1)S(1)}, bf16[1024,128]{1,0:T(8,128)(2,1)S(1)}, u32[]{:S(2)}, u32[]{:S(2)}) collective-permute-start(bf16[1024,128]{1,0:T(8,128)(2,1)S(1)} %bitcast.3), channel_id=1, source_target_pairs={{0,6},{1,7},{2,4},{3,5},{4,2},{5,3},{6,0},{7,1},{8,14},{9,15},{10,... | collective-permute-start | bytes 786440 | tf_op jit(solution)/shard_map/ppermute | solution.py:23
  31.3 22.9 %collective-permute-start.10 = (bf16[1024,128]{1,0:T(8,128)(2,1)S(1)}, bf16[1024,128]{1,0:T(8,128)(2,1)S(1)}, u32[]{:S(2)}, u32[]{:S(2)}) collective-permute-start(bf16[1024,128]{1,0:T(8,128)(2,1)S(1)} %bitcast.4), channel_id=1, source_target_pairs={{0,4},{1,5},{2,6},{3,7},{4,0},{5,1},{6,2},{7,3},{8,12},{9,13},{10,... | collective-permute-start | bytes 786440 | tf_op jit(solution)/shard_map/ppermute | solution.py:23
  33.9 20.3 %collective-permute-start.8 = (bf16[1024,128]{1,0:T(8,128)(2,1)S(1)}, bf16[1024,128]{1,0:T(8,128)(2,1)S(1)}, u32[]{:S(2)}, u32[]{:S(2)}) collective-permute-start(bf16[1024,128]{1,0:T(8,128)(2,1)S(1)} %bitcast.5), channel_id=1, source_target_pairs={{0,2},{1,3},{2,0},{3,1},{4,6},{5,7},{6,4},{7,5},{8,10},{9,11},{10,... | collective-permute-start | bytes 786440 | tf_op jit(solution)/shard_map/ppermute | solution.py:23
  35.3 19.3 %collective-permute-start.7 = (bf16[1024,128]{1,0:T(8,128)(2,1)S(1)}, bf16[1024,128]{1,0:T(8,128)(2,1)S(1)}, u32[]{:S(2)}, u32[]{:S(2)}) collective-permute-start(bf16[1024,128]{1,0:T(8,128)(2,1)S(1)} %bitcast.6), channel_id=1, source_target_pairs={{0,1},{1,0},{2,3},{3,2},{4,5},{5,4},{6,7},{7,6},{8,9},{9,8},{10,11... | collective-permute-start | bytes 786440 | tf_op jit(solution)/shard_map/ppermute | solution.py:23
  51.7 3.0 %collective-permute-start.13 = (bf16[1024,128]{1,0:T(8,128)(2,1)S(1)}, bf16[1024,128]{1,0:T(8,128)(2,1)S(1)}, u32[]{:S(2)}, u32[]{:S(2)}) collective-permute-start(bf16[1024,128]{1,0:T(8,128)(2,1)S(1)} %collective-permute-done.12.refs_10_), channel_id=1, source_target_pairs={{0,1},{1,0},{2,3},{3,2},{4,5},{5,4},{6,7},{7,6},{8,9},{9,8},{10,11... | collective-permute-start | bytes 786440 | tf_op jit(solution)/shard_map/ppermute | solution.py:23
  54.1 1.5 %collective-permute-start.11 = (bf16[1024,128]{1,0:T(8,128)(2,1)S(1)}, bf16[1024,128]{1,0:T(8,128)(2,1)S(1)}, u32[]{:S(2)}, u32[]{:S(2)}) collective-permute-start(bf16[1024,128]{1,0:T(8,128)(2,1)S(1)} %collective-permute-done.10.refs_8_), channel_id=1, source_target_pairs={{0,1},{1,0},{2,3},{3,2},{4,5},{5,4},{6,7},{7,6},{8,9},{9,8},{10,11... | collective-permute-start | bytes 786440 | tf_op jit(solution)/shard_map/ppermute | solution.py:23
  54.1 1.9 %collective-permute-start.9 = (bf16[1024,128]{1,0:T(8,128)(2,1)S(1)}, bf16[1024,128]{1,0:T(8,128)(2,1)S(1)}, u32[]{:S(2)}, u32[]{:S(2)}) collective-permute-start(bf16[1024,128]{1,0:T(8,128)(2,1)S(1)} %collective-permute-done.8.refs_6_), channel_id=1, source_target_pairs={{0,1},{1,0},{2,3},{3,2},{4,5},{5,4},{6,7},{7,6},{8,9},{9,8},{10,11... | collective-permute-start | bytes 786440 | tf_op jit(solution)/shard_map/ppermute | solution.py:23
  54.7 1.4 %copy-start.6 = (bf16[1024,128]{1,0:T(8,128)(2,1)}, bf16[1024,128]{1,0:T(8,128)(2,1)S(1)}, u32[]{:S(2)}) copy-start(bf16[1024,128]{1,0:T(8,128)(2,1)S(1)} %collective-permute-done.13.refs_11_) | copy-start | bytes 786436
  63.7 4.6 %collective-permute-start.14 = (f32[128,128]{1,0:T(8,128)S(1)}, f32[128,128]{1,0:T(8,128)S(1)}, u32[]{:S(2)}, u32[]{:S(2)}) collective-permute-start(f32[128,128]{1,0:T(8,128)S(1)} %get-tuple-element.20), channel_id=1, source_target_pairs={{0,1},{1,0},{2,3},{3,2},{4,5},{5,4},{6,7},{7,6},{8,9},{9,8},{10,11... | collective-permute-start | bytes 196616 | tf_op jit(solution)/shard_map/ppermute | solution.py:23
  67.4 20.6 %collective-permute-start.19 = (bf16[1024,128]{1,0:T(8,128)(2,1)S(1)}, bf16[1024,128]{1,0:T(8,128)(2,1)S(1)}, u32[]{:S(2)}, u32[]{:S(2)}) collective-permute-start(bf16[1024,128]{1,0:T(8,128)(2,1)S(1)} %get-tuple-element.22), channel_id=1, source_target_pairs={{0,8},{8,0},{16,24},{24,16},{1,9},{9,1},{17,25},{25,17},{2,10},{10... | collective-permute-start | bytes 786440 | tf_op jit(solution)/shard_map/ppermute | solution.py:23
  68.3 6.3 %collective-permute-start.15 = (f32[128,128]{1,0:T(8,128)S(1)}, f32[128,128]{1,0:T(8,128)S(1)}, u32[]{:S(2)}, u32[]{:S(2)}) collective-permute-start(f32[128,128]{1,0:T(8,128)S(1)} %add.15), channel_id=1, source_target_pairs={{0,2},{1,3},{2,0},{3,1},{4,6},{5,7},{6,4},{7,5},{8,10},{9,11},{10,... | collective-permute-start | bytes 196616 | tf_op jit(solution)/shard_map/ppermute | solution.py:23
  74.6 5.2 %collective-permute-start.16 = (f32[128,128]{1,0:T(8,128)S(1)}, f32[128,128]{1,0:T(8,128)S(1)}, u32[]{:S(2)}, u32[]{:S(2)}) collective-permute-start(f32[128,128]{1,0:T(8,128)S(1)} %add.16), channel_id=1, source_target_pairs={{0,4},{1,5},{2,6},{3,7},{4,0},{5,1},{6,2},{7,3},{8,12},{9,13},{10,... | collective-permute-start | bytes 196616 | tf_op jit(solution)/shard_map/ppermute | solution.py:23
  76.1 13.4 %collective-permute-start.20 = (bf16[1024,128]{1,0:T(8,128)(2,1)S(1)}, bf16[1024,128]{1,0:T(8,128)(2,1)S(1)}, u32[]{:S(2)}, u32[]{:S(2)}) collective-permute-start(bf16[1024,128]{1,0:T(8,128)(2,1)S(1)} %get-tuple-element.23), channel_id=1, source_target_pairs={{0,16},{8,24},{16,0},{24,8},{1,17},{9,25},{17,1},{25,9},{2,18},{10... | collective-permute-start | bytes 786440 | tf_op jit(solution)/shard_map/ppermute | solution.py:23
  79.9 8.1 %collective-permute-start.17 = (f32[128,128]{1,0:T(8,128)S(1)}, f32[128,128]{1,0:T(8,128)S(1)}, u32[]{:S(2)}, u32[]{:S(2)}) collective-permute-start(f32[128,128]{1,0:T(8,128)S(1)} %add.17), channel_id=1, source_target_pairs={{0,8},{8,0},{16,24},{24,16},{1,9},{9,1},{17,25},{25,17},{2,10},{10... | collective-permute-start | bytes 196616 | tf_op jit(solution)/shard_map/ppermute | solution.py:23
  80.7 10.3 %collective-permute-start.21 = (bf16[1024,128]{1,0:T(8,128)(2,1)S(1)}, bf16[1024,128]{1,0:T(8,128)(2,1)S(1)}, u32[]{:S(2)}, u32[]{:S(2)}) collective-permute-start(bf16[1024,128]{1,0:T(8,128)(2,1)S(1)} %get-tuple-element.24), channel_id=1, source_target_pairs={{0,24},{8,16},{16,8},{24,0},{1,25},{9,17},{17,9},{25,1},{2,26},{10... | collective-permute-start | bytes 786440 | tf_op jit(solution)/shard_map/ppermute | solution.py:23
  82.3 1.0 copy-start.5
  85.8 11.3 %collective-permute-start.4 = (bf16[1024,128]{1,0:T(8,128)(2,1)}, bf16[1024,128]{1,0:T(8,128)(2,1)S(1)}, u32[]{:S(2)}, u32[]{:S(2)}) collective-permute-start(bf16[1024,128]{1,0:T(8,128)(2,1)} %get-tuple-element.17), channel_id=1, source_target_pairs={{0,2},{1,3},{2,0},{3,1},{4,6},{5,7},{6,4},{7,5},{8,10},{9,11},{10,... | collective-permute-start | bytes 786440 | tf_op jit(solution)/shard_map/ppermute | solution.py:23
  88.0 18.3 %collective-permute-start.5 = (bf16[1024,128]{1,0:T(8,128)(2,1)}, bf16[1024,128]{1,0:T(8,128)(2,1)S(1)}, u32[]{:S(2)}, u32[]{:S(2)}) collective-permute-start(bf16[1024,128]{1,0:T(8,128)(2,1)} %get-tuple-element.18), channel_id=1, source_target_pairs={{0,4},{1,5},{2,6},{3,7},{4,0},{5,1},{6,2},{7,3},{8,12},{9,13},{10,... | collective-permute-start | bytes 786440 | tf_op jit(solution)/shard_map/ppermute | solution.py:23
  88.0 3.0 %copy-start.7 = (bf16[1024,128]{1,0:T(8,128)(2,1)}, bf16[1024,128]{1,0:T(8,128)(2,1)S(1)}, u32[]{:S(2)}) copy-start(bf16[1024,128]{1,0:T(8,128)(2,1)S(1)} %collective-permute-done.19.refs_1_) | copy-start | bytes 786436
  88.0 23.6 %collective-permute-start.6 = (bf16[1024,128]{1,0:T(8,128)(2,1)}, bf16[1024,128]{1,0:T(8,128)(2,1)S(1)}, u32[]{:S(2)}, u32[]{:S(2)}) collective-permute-start(bf16[1024,128]{1,0:T(8,128)(2,1)} %get-tuple-element.19), channel_id=1, source_target_pairs={{0,6},{1,7},{2,4},{3,5},{4,2},{5,3},{6,0},{7,1},{8,14},{9,15},{10,... | collective-permute-start | bytes 786440 | tf_op jit(solution)/shard_map/ppermute | solution.py:23
  89.5 1.5 %copy-start.8 = (bf16[1024,128]{1,0:T(8,128)(2,1)}, bf16[1024,128]{1,0:T(8,128)(2,1)S(1)}, u32[]{:S(2)}) copy-start(bf16[1024,128]{1,0:T(8,128)(2,1)S(1)} %collective-permute-done.20.refs_2_) | copy-start | bytes 786436
  89.5 4.5 %collective-permute-start.18 = (f32[128,128]{1,0:T(8,128)S(1)}, f32[128,128]{1,0:T(8,128)S(1)}, u32[]{:S(2)}, u32[]{:S(2)}) collective-permute-start(f32[128,128]{1,0:T(8,128)S(1)} %add.18), channel_id=1, source_target_pairs={{0,16},{8,24},{16,0},{24,8},{1,17},{9,25},{17,1},{25,9},{2,18},{10... | collective-permute-start | bytes 196616 | tf_op jit(solution)/shard_map/ppermute | solution.py:23
  91.0 0.7 copy-start.9
  97.1 14.5 %copy-start.10 = (bf16[1024,128]{1,0:T(8,128)(2,1)}, bf16[1024,128]{1,0:T(8,128)(2,1)S(1)}, u32[]{:S(2)}) copy-start(bf16[1024,128]{1,0:T(8,128)(2,1)S(1)} %collective-permute-done.4.refs_1_) | copy-start | bytes 786436
  106.3 5.3 %copy-start.11 = (bf16[1024,128]{1,0:T(8,128)(2,1)}, bf16[1024,128]{1,0:T(8,128)(2,1)S(1)}, u32[]{:S(2)}) copy-start(bf16[1024,128]{1,0:T(8,128)(2,1)S(1)} %collective-permute-done.5.refs_2_) | copy-start | bytes 786436
  111.6 0.7 copy-start.12
  (3 other events, 2.0 us)

commit v2 on v1

v2 whole, which is shorter than its diff:
```python
import functools
import math

import jax
import jax.numpy as jnp
from jax import lax
from jax.experimental import pallas as pl
from jax.experimental.pallas import tpu as pltpu
from jax.sharding import PartitionSpec as P

CORES = 2
MIB = 2**20
UNROLL = 23
WORK = 20
F32 = jnp.float32
BF16 = jnp.bfloat16
ANY = pl.BlockSpec(memory_space=pl.ANY)
SMEM = pl.BlockSpec(memory_space=pltpu.SMEM)
VMEM = pl.BlockSpec(memory_space=pltpu.VMEM)


def swap(value, axis, step):
    size = lax.axis_size(axis)
    return lax.ppermute(value, axis, [(i, i ^ step) for i in range(size)])


def room(size):
    return pltpu.CompilerParams(vmem_limit_bytes=size * MIB)


def cost(flops, moved):
    return pl.CostEstimate(flops=flops, bytes_accessed=moved, transcendentals=0)


def load_kernel(count_ref, tiles, held, sems):
    chunk = held.shape[0] // sems.shape[0]
    chunks = pl.cdiv(count_ref[0, 0], chunk)

    def copy(i):
        span = pl.ds(i * chunk, chunk)
        return pltpu.make_async_copy(tiles.at[0, 0, span], held.at[span], sems.at[i])

    @pl.loop(0, chunks)
    def _(i):
        copy(i).start()

    @pl.loop(0, chunks)
    def _(i):
        copy(i).wait()


def for_slots(live, slots, work):
    unroll = math.gcd(slots, UNROLL)

    @pl.loop(0, pl.cdiv(live, unroll))
    def _(i):
        for j in range(unroll):
            work(i * unroll + j)


def forward_kernel(n_shards, count_ref, rows_ref, cols_ref, tiles, *refs):
    shards, (keep, send) = refs[:n_shards], refs[n_shards : n_shards + 2]
    panel, acc = refs[n_shards + 2 :]
    slots, tile = tiles.shape[:2]
    own = shards[0].shape[0]
    dump = acc.shape[0] - 1
    live = count_ref[0, 0]
    row, col = lax.axis_index("row"), lax.axis_index("col")
    line, core = col // CORES, col % CORES

    acc[...] = jnp.zeros_like(acc)
    for k in range(n_shards):
        panel[pl.ds(pl.multiple_of((row ^ k) * own, own), own), :] = shards[k][...]

    def work(s):
        c = cols_ref[0, 0, s]
        r = jnp.where(s < live, rows_ref[0, 0, s], dump)
        source = panel[pl.ds(pl.multiple_of(c * tile, tile), tile), :]
        acc[r] += jnp.dot(tiles[s], source, preferred_element_type=F32)

    for_slots(live, slots, work)
    per = own // tile
    for k in range(keep.shape[0] // own):
        base = (line ^ k) * CORES
        for b in range(per):
            span = pl.ds(k * own + b * tile, tile)
            keep[span, :] = acc[(base + core) * per + b].astype(BF16)
            send[span, :] = acc[(base + 1 - core) * per + b].astype(BF16)


def backward_kernel(n_rows, n_lines, count_ref, rows_ref, cols_ref, tiles, scale, *refs):
    n_cots = n_lines * CORES
    hids, cots, refs = refs[:n_rows], refs[n_rows : n_rows + n_cots], refs[n_rows + n_cots :]
    outs, weight_term, refs = refs[:n_rows], refs[n_rows], refs[n_rows + 1 :]
    turned, acc = refs
    slots, tile = tiles.shape[:2]
    own = hids[0].shape[0]
    per = own // tile
    dump = acc.shape[0] - 1
    live = count_ref[0, 0]
    row, col = lax.axis_index("row"), lax.axis_index("col")
    line, core = col // CORES, col % CORES

    acc[...] = jnp.zeros_like(acc)
    for k in range(n_cots):
        place = ((line ^ (k // CORES)) * CORES + (core ^ (k % CORES))) * per
        for b in range(per):
            turned[place + b] = cots[k][b * tile : (b + 1) * tile, :].T

    def work(s):
        r = rows_ref[0, 0, s]
        c = jnp.where(s < live, cols_ref[0, 0, s], dump)
        acc[c] += jnp.dot(turned[r], tiles[s], preferred_element_type=F32)

    for_slots(live, slots, work)
    total = jnp.zeros(weight_term.shape, F32)
    for k in range(n_rows):
        for b in range(per):
            span = pl.ds(b * tile, tile)
            part = acc[(row ^ k) * per + b]
            total += jnp.dot(part.astype(BF16), hids[k][span, :], preferred_element_type=F32)
            outs[k][span, :] = part.T.astype(BF16)
    weight_term[...] = total.T * scale[0]


def pair_kernel(keep, got, *outs):
    own = outs[0].shape[0]
    for k, out in enumerate(outs):
        span = pl.ds(k * own, own)
        out[...] = (keep[span, :].astype(F32) + got[span, :].astype(F32)).astype(BF16)


def summed(parts):
    total = parts[0][...].astype(F32)
    for part in parts[1:]:
        total += part[...].astype(F32)
    return total.astype(BF16)


def out_kernel(weight, *refs):
    refs[-1][0] = jnp.dot(summed(refs[:-1]), weight[...], preferred_element_type=F32).astype(BF16)


def grad_kernel(weight, mask, *refs):
    turned = lax.dot_general(
        summed(refs[:-1]), weight[...], (((1,), (1,)), ((), ())), preferred_element_type=F32
    )
    refs[-1][0] = (turned * mask[0].astype(F32)).astype(BF16)


def body(features, relu_mask, tiles, tile_rows, tile_cols, tile_count, weight, cotangent):
    slots, tile = tiles.shape[2:4]
    own, width = features.shape[1:]
    n_rows, n_cols = lax.axis_size("row"), lax.axis_size("col")
    n_lines = n_cols // CORES
    row_blocks, col_blocks = own * n_cols // tile, own * n_rows // tile
    ids = (tile_count, tile_rows, tile_cols)
    block = jax.ShapeDtypeStruct((own, width), BF16)
    work = 2 * tiles.size * width

    cot = cotangent[0]
    cots = [cot] + [swap(cot, "col", CORES * k) for k in range(1, n_lines)]
    cots = [part for mine in cots for part in (mine, swap(mine, "col", 1))]
    hidden = features[0] * relu_mask[0].astype(BF16)
    hids = [hidden] + [swap(hidden, "row", k) for k in range(1, n_rows)]

    held = pl.pallas_call(
        load_kernel,
        out_shape=jax.ShapeDtypeStruct((slots, tile, tile), BF16),
        in_specs=[SMEM, ANY],
        out_specs=VMEM,
        scratch_shapes=[pltpu.SemaphoreType.DMA((slots // math.gcd(slots, 8),))],
        compiler_params=room(WORK),
        cost_estimate=cost(0, 2 * tiles.size),
        name="load_tiles",
    )(tile_count, tiles)

    half = jax.ShapeDtypeStruct((n_lines * own, width), BF16)
    keep, send = pl.pallas_call(
        functools.partial(forward_kernel, n_rows),
        out_shape=(half, half),
        in_specs=[SMEM] * 3 + [VMEM] * (1 + n_rows),
        out_specs=(VMEM, VMEM),
        scratch_shapes=[
            pltpu.VMEM((n_rows * own, width), BF16),
            pltpu.VMEM((row_blocks + 1, tile, width), F32),
        ],
        compiler_params=room(WORK),
        cost_estimate=cost(work, 2 * tiles.size),
        name="forward_tiles",
    )(*ids, held, *hids)
    got = swap(send, "col", 1)
    pairs = pl.pallas_call(
        pair_kernel,
        out_shape=(block,) * n_lines,
        in_specs=[VMEM] * 2,
        out_specs=(VMEM,) * n_lines,
        compiler_params=room(8),
        name="pair_sum",
    )(keep, got)
    parts = [pairs[0]] + [swap(pairs[k], "col", CORES * k) for k in range(1, n_lines)]
    out_pre = pl.pallas_call(
        out_kernel,
        out_shape=jax.ShapeDtypeStruct((1, own, width), BF16),
        in_specs=[VMEM] * (1 + n_lines),
        out_specs=VMEM,
        compiler_params=room(8),
        name="out_pre",
    )(weight, *parts)

    scale = 1.0 / jnp.sqrt(jnp.full((1,), own * n_rows * n_cols, F32))
    *backs, weight_term = pl.pallas_call(
        functools.partial(backward_kernel, n_rows, n_lines),
        out_shape=(block,) * n_rows + (jax.ShapeDtypeStruct((width, width), F32),),
        in_specs=[SMEM] * 3 + [VMEM] + [SMEM] + [VMEM] * (n_rows + n_cols),
        out_specs=(VMEM,) * (n_rows + 1),
        scratch_shapes=[
            pltpu.VMEM((row_blocks, width, tile), BF16),
            pltpu.VMEM((col_blocks + 1, width, tile), F32),
        ],
        compiler_params=room(WORK),
        cost_estimate=cost(work, 2 * tiles.size),
        name="backward_tiles",
    )(*ids, held, scale, *hids, *cots)
    backs = [backs[0]] + [swap(backs[k], "row", k) for k in range(1, n_rows)]
    input_grad = pl.pallas_call(
        grad_kernel,
        out_shape=jax.ShapeDtypeStruct((1, own, width), BF16),
        in_specs=[VMEM] * (2 + n_rows),
        out_specs=VMEM,
        compiler_params=room(8),
        name="input_grad",
    )(weight, relu_mask, *backs)

    for axis, size in (("col", n_cols), ("row", n_rows)):
        for bit in range(size.bit_length() - 1):
            weight_term = weight_term + swap(weight_term, axis, 1 << bit)
    return (out_pre, weight_term, input_grad)


def solution(mesh):
    placed = (
        P("col", "row", None),
        P("col", "row", None),
        P("row", "col", None, None, None),
        P("row", "col", None),
        P("row", "col", None),
        P("row", "col"),
        P(),
        P("row", "col", None),
    )
    return jax.shard_map(
        body,
        mesh=mesh,
        in_specs=placed,
        out_specs=(P("row", "col", None), P(), P("col", "row", None)),
        check_vma=False,
    )
```

time: 115 us -> 79.7 us (0.69)
  the two profiles are of different devices: /device:TPU:8 before, /device:TPU:0 now
where the time goes in v2:
time: 79.7 us; the launch traced here: 78.8 us
  starting transfers between devices  26.7 us (34%)
  Pallas kernels  26.2 us (33%)
  waiting for transfers between devices  22.6 us (28%)
  other arithmetic  1.84 us (2%)
  between operations  1.46 us (2%)
    ppermute x22, starting transfers between devices, swap(): return lax.ppermute(value, axis, [(i, i ^ step) for i in range(size)])  26.7 us
    ppermute x22, waiting for transfers between devices, swap(): return lax.ppermute(value, axis, [(i, i ^ step) for i in range(size)])  22.6 us
    pallas_call x1, Pallas kernels, body(): pl.pallas_call(functools.partial(forward_kernel, n_rows), out_shape=(half...  8.73 us
    pallas_call x1, Pallas kernels, body(): pl.pallas_call(load_kernel, out_shape=jax.ShapeDtypeStruct((slots, tile,...  8.15 us
    pallas_call x1, Pallas kernels, body(): pl.pallas_call(functools.partial(backward_kernel, n_rows, n_lines), out_s...  7.14 us
  transfers between devices with their start and end apart: 22, of which 12 were waited for; matrix products, arithmetic and copies ran while one was open for 1% of the time, Pallas kernels for 32%

profile of v2, /device:TPU:0, one launch (start us, length us, event | category | flops | bytes accessed | tf_op | source)
XLA Modules:
  0.0 78.8 jit_solution(17613581240278537589)
XLA Ops:
  0.6 1.2 %multiply_bitcast_fusion.refs_0_ = bf16[1024,128]{1,0:T(8,128)(2,1)S(1)} fusion(bf16[1,1024,128]{2,1,0:T(8,128)(2,1)} %param.8, s32[1,1024,128]{2,1,0:T(8,128)} %mask.1), kind=kLoop, calls=%fused_computation | loop fusion | flops 262144 | bytes 1048576 | tf_op jit(solution)/shard_map/mul | solution.py:164
  1.8 3.0 %collective-permute-start = (bf16[1024,128]{1,0:T(8,128)(2,1)S(1)}, bf16[1024,128]{1,0:T(8,128)(2,1)S(1)}, u32[]{:S(2)}, u32[]{:S(2)}) collective-permute-start(bf16[1024,128]{1,0:T(8,128)(2,1)S(1)} %multiply_bitcast_fusion.refs_0_), channel_id=1, source_target_pairs={{0,8},{8,0},{16,24},{24,16},{1,9},{9,1},{17,25},{25,17},{2,10},{10... | collective-permute-start | bytes 786440 | tf_op jit(solution)/shard_map/ppermute | solution.py:24
  4.8 1.5 %collective-permute-start.1 = (bf16[1024,128]{1,0:T(8,128)(2,1)S(1)}, bf16[1024,128]{1,0:T(8,128)(2,1)S(1)}, u32[]{:S(2)}, u32[]{:S(2)}) collective-permute-start(bf16[1024,128]{1,0:T(8,128)(2,1)S(1)} %multiply_bitcast_fusion.refs_0_), channel_id=1, source_target_pairs={{0,16},{8,24},{16,0},{24,8},{1,17},{9,25},{17,1},{25,9},{2,18},{10... | collective-permute-start | bytes 786440 | tf_op jit(solution)/shard_map/ppermute | solution.py:24
  6.3 3.0 %collective-permute-start.10 = (bf16[1024,128]{1,0:T(8,128)(2,1)}, bf16[1024,128]{1,0:T(8,128)(2,1)S(1)}, u32[]{:S(2)}, u32[]{:S(2)}) collective-permute-start(bf16[1024,128]{1,0:T(8,128)(2,1)} %bitcast.3), channel_id=1, source_target_pairs={{0,4},{1,5},{2,6},{3,7},{4,0},{5,1},{6,2},{7,3},{8,12},{9,13},{10,... | collective-permute-start | bytes 786440 | tf_op jit(solution)/shard_map/ppermute | solution.py:24
  9.4 1.3 %collective-permute-start.12 = (bf16[1024,128]{1,0:T(8,128)(2,1)}, bf16[1024,128]{1,0:T(8,128)(2,1)S(1)}, u32[]{:S(2)}, u32[]{:S(2)}) collective-permute-start(bf16[1024,128]{1,0:T(8,128)(2,1)} %bitcast.4), channel_id=1, source_target_pairs={{0,6},{1,7},{2,4},{3,5},{4,2},{5,3},{6,0},{7,1},{8,14},{9,15},{10,... | collective-permute-start | bytes 786440 | tf_op jit(solution)/shard_map/ppermute | solution.py:24
  11.4 8.2 %load_tiles.1.tiles = bf16[184,256,256]{2,1,0:T(8,128)(2,1)S(1)} custom-call(s32[1,1]{1,0:T(1,128)S(6)} %copy.11.count_ref, bf16[1,1,184,256,256]{4,3,2,1,0:T(8,128)(2,1)} %tiles.1), custom_call_target="tpu_custom_call" | custom-call | bytes 24117248 | tf_op jit(solution)/shard_map/load_tiles/pallas_call | solution.py:167
  19.7 8.7 %forward_tiles.1 = (bf16[4096,128]{1,0:T(8,128)(2,1)S(1)}, bf16[4096,128]{1,0:T(8,128)(2,1)S(1)}) custom-call(s32[1,1]{1,0:T(1,128)S(6)} %copy.11.count_ref, s32[1,1,184]{2,1,0:T(1,128)S(1)} %copy-done.3, s32[1,1,184]{2,1,0:T(1,128)S(1)} %copy-done.4, bf16[184,256,256]{2,1,0:T(8,128)(2,1)S(1)} %load_tiles.1.tiles, ...), custom_call_target="tpu_custom_call" | custom-call | flops 3087007744 | bytes 24117248 | tf_op jit(solution)/shard_map/forward_tiles/pallas_call | solution.py:179
  28.6 0.5 collective-permute-start.7
  29.1 0.4 collective-permute-start.13
  29.6 1.9 %collective-permute-done.8.refs_6_ = bf16[1024,128]{1,0:T(8,128)(2,1)S(1)} collective-permute-done((bf16[1024,128]{1,0:T(8,128)(2,1)S(1)}, bf16[1024,128]{1,0:T(8,128)(2,1)S(1)}, u32[]{:S(2)}, u32[]{:S(2)}) %collective-permute-start.8) | collective-permute-done | bytes 262176 | tf_op jit(solution)/shard_map/ppermute | solution.py:24
  31.6 0.4 collective-permute-done.11.refs_9_
  32.3 0.7 collective-permute-done.9.refs_7_
  33.0 7.1 %backward_tiles.1 = (bf16[1024,128]{1,0:T(8,128)(2,1)S(1)}, bf16[1024,128]{1,0:T(8,128)(2,1)S(1)}, bf16[1024,128]{1,0:T(8,128)(2,1)S(1)}, bf16[1024,128]{1,0:T(8,128)(2,1)S(1)}, f32[128,128]{1,0:T(8,128)S(1)}) custom-call(s32[1,1]{1,0:T(1,128)S(6)} %copy.11.count_ref, s32[1,1,184]{2,1,0:T(1,128)S(1)} %copy-done.3, s32[1,1,184]{2,1,0:T(1,128)S(1)} %copy-done.4, ...), custom_call_target="tpu_custom_call" | custom-call | flops 3087007744 | bytes 24117248 | tf_op jit(solution)/shard_map/backward_tiles/pallas_call | solution.py:212
  40.3 1.2 %collective-permute-done.14 = f32[128,128]{1,0:T(8,128)S(1)} collective-permute-done((f32[128,128]{1,0:T(8,128)S(1)}, f32[128,128]{1,0:T(8,128)S(1)}, u32[]{:S(2)}, u32[]{:S(2)}) %collective-permute-start.14) | collective-permute-done | bytes 65568 | tf_op jit(solution)/shard_map/ppermute | solution.py:24
  41.5 2.1 %collective-permute-start.15 = (f32[128,128]{1,0:T(8,128)S(1)}, f32[128,128]{1,0:T(8,128)S(1)}, u32[]{:S(2)}, u32[]{:S(2)}) collective-permute-start(f32[128,128]{1,0:T(8,128)S(1)} %add.15), channel_id=1, source_target_pairs={{0,2},{1,3},{2,0},{3,1},{4,6},{5,7},{6,4},{7,5},{8,10},{9,11},{10,... | collective-permute-start | bytes 196616 | tf_op jit(solution)/shard_map/ppermute | solution.py:24
  43.6 2.2 %collective-permute-done.15 = f32[128,128]{1,0:T(8,128)S(1)} collective-permute-done((f32[128,128]{1,0:T(8,128)S(1)}, f32[128,128]{1,0:T(8,128)S(1)}, u32[]{:S(2)}, u32[]{:S(2)}) %collective-permute-start.15) | collective-permute-done | bytes 65568 | tf_op jit(solution)/shard_map/ppermute | solution.py:24
  45.9 3.9 %collective-permute-start.16 = (f32[128,128]{1,0:T(8,128)S(1)}, f32[128,128]{1,0:T(8,128)S(1)}, u32[]{:S(2)}, u32[]{:S(2)}) collective-permute-start(f32[128,128]{1,0:T(8,128)S(1)} %add.16), channel_id=1, source_target_pairs={{0,4},{1,5},{2,6},{3,7},{4,0},{5,1},{6,2},{7,3},{8,12},{9,13},{10,... | collective-permute-start | bytes 196616 | tf_op jit(solution)/shard_map/ppermute | solution.py:24
  49.8 1.5 %collective-permute-start.20 = (bf16[1024,128]{1,0:T(8,128)(2,1)S(1)}, bf16[1024,128]{1,0:T(8,128)(2,1)S(1)}, u32[]{:S(2)}, u32[]{:S(2)}) collective-permute-start(bf16[1024,128]{1,0:T(8,128)(2,1)S(1)} %get-tuple-element.23), channel_id=1, source_target_pairs={{0,16},{8,24},{16,0},{24,8},{1,17},{9,25},{17,1},{25,9},{2,18},{10... | collective-permute-start | bytes 786440 | tf_op jit(solution)/shard_map/ppermute | solution.py:24
  51.2 1.5 %collective-permute-done.16 = f32[128,128]{1,0:T(8,128)S(1)} collective-permute-done((f32[128,128]{1,0:T(8,128)S(1)}, f32[128,128]{1,0:T(8,128)S(1)}, u32[]{:S(2)}, u32[]{:S(2)}) %collective-permute-start.16) | collective-permute-done | bytes 65568 | tf_op jit(solution)/shard_map/ppermute | solution.py:24
  52.7 1.3 %collective-permute-start.17 = (f32[128,128]{1,0:T(8,128)S(1)}, f32[128,128]{1,0:T(8,128)S(1)}, u32[]{:S(2)}, u32[]{:S(2)}) collective-permute-start(f32[128,128]{1,0:T(8,128)S(1)} %add.17), channel_id=1, source_target_pairs={{0,8},{8,0},{16,24},{24,16},{1,9},{9,1},{17,25},{25,17},{2,10},{10... | collective-permute-start | bytes 196616 | tf_op jit(solution)/shard_map/ppermute | solution.py:24
  54.0 1.0 %collective-permute-start.21 = (bf16[1024,128]{1,0:T(8,128)(2,1)S(1)}, bf16[1024,128]{1,0:T(8,128)(2,1)S(1)}, u32[]{:S(2)}, u32[]{:S(2)}) collective-permute-start(bf16[1024,128]{1,0:T(8,128)(2,1)S(1)} %get-tuple-element.24), channel_id=1, source_target_pairs={{0,24},{8,16},{16,8},{24,0},{1,25},{9,17},{17,9},{25,1},{2,26},{10... | collective-permute-start | bytes 786440 | tf_op jit(solution)/shard_map/ppermute | solution.py:24
  55.3 1.3 %collective-permute-start.4 = (bf16[1024,128]{1,0:T(8,128)(2,1)S(1)}, bf16[1024,128]{1,0:T(8,128)(2,1)S(1)}, u32[]{:S(2)}, u32[]{:S(2)}) collective-permute-start(bf16[1024,128]{1,0:T(8,128)(2,1)S(1)} %get-tuple-element.17), channel_id=1, source_target_pairs={{0,2},{1,3},{2,0},{3,1},{4,6},{5,7},{6,4},{7,5},{8,10},{9,11},{10,... | collective-permute-start | bytes 786440 | tf_op jit(solution)/shard_map/ppermute | solution.py:24
  56.6 1.1 %collective-permute-done.17 = f32[128,128]{1,0:T(8,128)S(1)} collective-permute-done((f32[128,128]{1,0:T(8,128)S(1)}, f32[128,128]{1,0:T(8,128)S(1)}, u32[]{:S(2)}, u32[]{:S(2)}) %collective-permute-start.17) | collective-permute-done | bytes 65568 | tf_op jit(solution)/shard_map/ppermute | solution.py:24
  57.7 2.2 %collective-permute-start.5 = (bf16[1024,128]{1,0:T(8,128)(2,1)S(1)}, bf16[1024,128]{1,0:T(8,128)(2,1)S(1)}, u32[]{:S(2)}, u32[]{:S(2)}) collective-permute-start(bf16[1024,128]{1,0:T(8,128)(2,1)S(1)} %get-tuple-element.18), channel_id=1, source_target_pairs={{0,4},{1,5},{2,6},{3,7},{4,0},{5,1},{6,2},{7,3},{8,12},{9,13},{10,... | collective-permute-start | bytes 786440 | tf_op jit(solution)/shard_map/ppermute | solution.py:24
  60.0 0.6 collective-permute-start.6
  60.6 1.6 %collective-permute-done.20.refs_2_ = bf16[1024,128]{1,0:T(8,128)(2,1)S(1)} collective-permute-done((bf16[1024,128]{1,0:T(8,128)(2,1)S(1)}, bf16[1024,128]{1,0:T(8,128)(2,1)S(1)}, u32[]{:S(2)}, u32[]{:S(2)}) %collective-permute-start.20) | collective-permute-done | bytes 262176 | tf_op jit(solution)/shard_map/ppermute | solution.py:24
  62.2 2.5 %collective-permute-start.18 = (f32[128,128]{1,0:T(8,128)S(1)}, f32[128,128]{1,0:T(8,128)S(1)}, u32[]{:S(2)}, u32[]{:S(2)}) collective-permute-start(f32[128,128]{1,0:T(8,128)S(1)} %add.18), channel_id=1, source_target_pairs={{0,16},{8,24},{16,0},{24,8},{1,17},{9,25},{17,1},{25,9},{2,18},{10... | collective-permute-start | bytes 196616 | tf_op jit(solution)/shard_map/ppermute | solution.py:24
  64.7 1.0 %input_grad.1 = bf16[1,1024,128]{2,1,0:T(8,128)(2,1)} custom-call(bf16[128,128]{1,0:T(8,128)(2,1)S(1)} %copy-done.2, s32[1,1024,128]{2,1,0:T(8,128)S(1)} %copy-done, bf16[1024,128]{1,0:T(8,128)(2,1)S(1)} %get-tuple-element.21.refs_0_, bf16[1024,128]{1,0:T(8,128)(2,1)S(1)} %collective-permute-done.19.refs_1_, ...), custom_call_target="tpu_custom_call" | custom-call | tf_op jit(solution)/shard_map/input_grad/pallas_call | solution.py:226
  65.7 1.3 %collective-permute-done.18 = f32[128,128]{1,0:T(8,128)S(1)} collective-permute-done((f32[128,128]{1,0:T(8,128)S(1)}, f32[128,128]{1,0:T(8,128)S(1)}, u32[]{:S(2)}, u32[]{:S(2)}) %collective-permute-start.18) | collective-permute-done | bytes 65568 | tf_op jit(solution)/shard_map/ppermute | solution.py:24
  66.9 0.6 add.19
  67.6 10.3 %collective-permute-done.5.refs_2_ = bf16[1024,128]{1,0:T(8,128)(2,1)S(1)} collective-permute-done((bf16[1024,128]{1,0:T(8,128)(2,1)S(1)}, bf16[1024,128]{1,0:T(8,128)(2,1)S(1)}, u32[]{:S(2)}, u32[]{:S(2)}) %collective-permute-start.5) | collective-permute-done | bytes 262176 | tf_op jit(solution)/shard_map/ppermute | solution.py:24
  77.9 1.0 %out_pre.1 = bf16[1,1024,128]{2,1,0:T(8,128)(2,1)} custom-call(bf16[128,128]{1,0:T(8,128)(2,1)S(1)} %copy-done.2, bf16[1024,128]{1,0:T(8,128)(2,1)S(1)} %get-tuple-element.16.refs_0_, bf16[1024,128]{1,0:T(8,128)(2,1)S(1)} %collective-permute-done.4.refs_1_, bf16[1024,128]{1,0:T(8,128)(2,1)S(1)} %collective-permute-done.5.refs_2_, ...), custom_call_target="tpu_custom_call" | custom-call | tf_op jit(solution)/shard_map/out_pre/pallas_call | solution.py:202
  (34 shorter events, 1.2 us)
Async XLA Ops:
  1.8 17.8 %collective-permute-start = (bf16[1024,128]{1,0:T(8,128)(2,1)S(1)}, bf16[1024,128]{1,0:T(8,128)(2,1)S(1)}, u32[]{:S(2)}, u32[]{:S(2)}) collective-permute-start(bf16[1024,128]{1,0:T(8,128)(2,1)S(1)} %multiply_bitcast_fusion.refs_0_), channel_id=1, source_target_pairs={{0,8},{8,0},{16,24},{24,16},{1,9},{9,1},{17,25},{25,17},{2,10},{10... | collective-permute-start | bytes 786440 | tf_op jit(solution)/shard_map/ppermute | solution.py:24
  4.8 14.9 %collective-permute-start.1 = (bf16[1024,128]{1,0:T(8,128)(2,1)S(1)}, bf16[1024,128]{1,0:T(8,128)(2,1)S(1)}, u32[]{:S(2)}, u32[]{:S(2)}) collective-permute-start(bf16[1024,128]{1,0:T(8,128)(2,1)S(1)} %multiply_bitcast_fusion.refs_0_), channel_id=1, source_target_pairs={{0,16},{8,24},{16,0},{24,8},{1,17},{9,25},{17,1},{25,9},{2,18},{10... | collective-permute-start | bytes 786440 | tf_op jit(solution)/shard_map/ppermute | solution.py:24
  6.3 13.4 %collective-permute-start.2 = (bf16[1024,128]{1,0:T(8,128)(2,1)S(1)}, bf16[1024,128]{1,0:T(8,128)(2,1)S(1)}, u32[]{:S(2)}, u32[]{:S(2)}) collective-permute-start(bf16[1024,128]{1,0:T(8,128)(2,1)S(1)} %multiply_bitcast_fusion.refs_0_), channel_id=1, source_target_pairs={{0,24},{8,16},{16,8},{24,0},{1,25},{9,17},{17,9},{25,1},{2,26},{10... | collective-permute-start | bytes 786440 | tf_op jit(solution)/shard_map/ppermute | solution.py:24
  6.3 22.7 %collective-permute-start.10 = (bf16[1024,128]{1,0:T(8,128)(2,1)}, bf16[1024,128]{1,0:T(8,128)(2,1)S(1)}, u32[]{:S(2)}, u32[]{:S(2)}) collective-permute-start(bf16[1024,128]{1,0:T(8,128)(2,1)} %bitcast.3), channel_id=1, source_target_pairs={{0,4},{1,5},{2,6},{3,7},{4,0},{5,1},{6,2},{7,3},{8,12},{9,13},{10,... | collective-permute-start | bytes 786440 | tf_op jit(solution)/shard_map/ppermute | solution.py:24
  9.4 19.8 %collective-permute-start.12 = (bf16[1024,128]{1,0:T(8,128)(2,1)}, bf16[1024,128]{1,0:T(8,128)(2,1)S(1)}, u32[]{:S(2)}, u32[]{:S(2)}) collective-permute-start(bf16[1024,128]{1,0:T(8,128)(2,1)} %bitcast.4), channel_id=1, source_target_pairs={{0,6},{1,7},{2,4},{3,5},{4,2},{5,3},{6,0},{7,1},{8,14},{9,15},{10,... | collective-permute-start | bytes 786440 | tf_op jit(solution)/shard_map/ppermute | solution.py:24
  11.4 8.2 %copy-start.1 = (bf16[1,1024,128]{2,1,0:T(8,128)(2,1)S(1)}, bf16[1,1024,128]{2,1,0:T(8,128)(2,1)}, u32[]{:S(2)}) copy-start(bf16[1,1024,128]{2,1,0:T(8,128)(2,1)} %param.15) | copy-start | bytes 786436
  11.4 8.3 %copy-start.3 = (s32[1,1,184]{2,1,0:T(1,128)S(1)}, s32[1,1,184]{2,1,0:T(1,128)}, u32[]{:S(2)}) copy-start(s32[1,1,184]{2,1,0:T(1,128)} %rows_ref.3) | copy-start | bytes 2212
  11.4 8.3 %copy-start.4 = (s32[1,1,184]{2,1,0:T(1,128)S(1)}, s32[1,1,184]{2,1,0:T(1,128)}, u32[]{:S(2)}) copy-start(s32[1,1,184]{2,1,0:T(1,128)} %cols_ref.3) | copy-start | bytes 2212
  19.6 45.1 %copy-start = (s32[1,1024,128]{2,1,0:T(8,128)S(1)}, s32[1,1024,128]{2,1,0:T(8,128)}, u32[]{:S(2)}) copy-start(s32[1,1024,128]{2,1,0:T(8,128)} %mask.1) | copy-start | bytes 1572868
  19.6 45.1 %copy-start.2 = (bf16[128,128]{1,0:T(8,128)(2,1)S(1)}, bf16[128,128]{1,0:T(8,128)(2,1)}, u32[]{:S(2)}) copy-start(bf16[128,128]{1,0:T(8,128)(2,1)} %weight.3) | copy-start | bytes 98308
  19.6 11.9 %collective-permute-start.8 = (bf16[1024,128]{1,0:T(8,128)(2,1)S(1)}, bf16[1024,128]{1,0:T(8,128)(2,1)S(1)}, u32[]{:S(2)}, u32[]{:S(2)}) collective-permute-start(bf16[1024,128]{1,0:T(8,128)(2,1)S(1)} %bitcast.5), channel_id=1, source_target_pairs={{0,2},{1,3},{2,0},{3,1},{4,6},{5,7},{6,4},{7,5},{8,10},{9,11},{10,... | collective-permute-start | bytes 786440 | tf_op jit(solution)/shard_map/ppermute | solution.py:24
  28.5 26.5 %collective-permute-start.3 = (bf16[4096,128]{1,0:T(8,128)(2,1)S(1)}, bf16[4096,128]{1,0:T(8,128)(2,1)S(1)}, u32[]{:S(2)}, u32[]{:S(2)}) collective-permute-start(bf16[4096,128]{1,0:T(8,128)(2,1)S(1)} %get-tuple-element.15), channel_id=1, source_target_pairs={{0,1},{1,0},{2,3},{3,2},{4,5},{5,4},{6,7},{7,6},{8,9},{9,8},{10,11... | collective-permute-start | bytes 3145736 | tf_op jit(solution)/shard_map/ppermute | solution.py:24
  28.6 3.0 %collective-permute-start.7 = (bf16[1024,128]{1,0:T(8,128)(2,1)S(1)}, bf16[1024,128]{1,0:T(8,128)(2,1)S(1)}, u32[]{:S(2)}, u32[]{:S(2)}) collective-permute-start(bf16[1024,128]{1,0:T(8,128)(2,1)S(1)} %bitcast.6), channel_id=1, source_target_pairs={{0,1},{1,0},{2,3},{3,2},{4,5},{5,4},{6,7},{7,6},{8,9},{9,8},{10,11... | collective-permute-start | bytes 786440 | tf_op jit(solution)/shard_map/ppermute | solution.py:24
  29.1 2.9 %collective-permute-start.11 = (bf16[1024,128]{1,0:T(8,128)(2,1)S(1)}, bf16[1024,128]{1,0:T(8,128)(2,1)S(1)}, u32[]{:S(2)}, u32[]{:S(2)}) collective-permute-start(bf16[1024,128]{1,0:T(8,128)(2,1)S(1)} %collective-permute-done.10.refs_8_), channel_id=1, source_target_pairs={{0,1},{1,0},{2,3},{3,2},{4,5},{5,4},{6,7},{7,6},{8,9},{9,8},{10,11... | collective-permute-start | bytes 786440 | tf_op jit(solution)/shard_map/ppermute | solution.py:24
  29.1 3.2 %collective-permute-start.13 = (bf16[1024,128]{1,0:T(8,128)(2,1)S(1)}, bf16[1024,128]{1,0:T(8,128)(2,1)S(1)}, u32[]{:S(2)}, u32[]{:S(2)}) collective-permute-start(bf16[1024,128]{1,0:T(8,128)(2,1)S(1)} %collective-permute-done.12.refs_10_), channel_id=1, source_target_pairs={{0,1},{1,0},{2,3},{3,2},{4,5},{5,4},{6,7},{7,6},{8,9},{9,8},{10,11... | collective-permute-start | bytes 786440 | tf_op jit(solution)/shard_map/ppermute | solution.py:24
  31.5 1.5 %collective-permute-start.9 = (bf16[1024,128]{1,0:T(8,128)(2,1)S(1)}, bf16[1024,128]{1,0:T(8,128)(2,1)S(1)}, u32[]{:S(2)}, u32[]{:S(2)}) collective-permute-start(bf16[1024,128]{1,0:T(8,128)(2,1)S(1)} %collective-permute-done.8.refs_6_), channel_id=1, source_target_pairs={{0,1},{1,0},{2,3},{3,2},{4,5},{5,4},{6,7},{7,6},{8,9},{9,8},{10,11... | collective-permute-start | bytes 786440 | tf_op jit(solution)/shard_map/ppermute | solution.py:24
  40.2 1.3 %collective-permute-start.14 = (f32[128,128]{1,0:T(8,128)S(1)}, f32[128,128]{1,0:T(8,128)S(1)}, u32[]{:S(2)}, u32[]{:S(2)}) collective-permute-start(f32[128,128]{1,0:T(8,128)S(1)} %get-tuple-element.20), channel_id=1, source_target_pairs={{0,1},{1,0},{2,3},{3,2},{4,5},{5,4},{6,7},{7,6},{8,9},{9,8},{10,11... | collective-permute-start | bytes 196616 | tf_op jit(solution)/shard_map/ppermute | solution.py:24
  40.3 19.7 %collective-permute-start.19 = (bf16[1024,128]{1,0:T(8,128)(2,1)S(1)}, bf16[1024,128]{1,0:T(8,128)(2,1)S(1)}, u32[]{:S(2)}, u32[]{:S(2)}) collective-permute-start(bf16[1024,128]{1,0:T(8,128)(2,1)S(1)} %get-tuple-element.22), channel_id=1, source_target_pairs={{0,8},{8,0},{16,24},{24,16},{1,9},{9,1},{17,25},{25,17},{2,10},{10... | collective-permute-start | bytes 786440 | tf_op jit(solution)/shard_map/ppermute | solution.py:24
  41.5 4.3 %collective-permute-start.15 = (f32[128,128]{1,0:T(8,128)S(1)}, f32[128,128]{1,0:T(8,128)S(1)}, u32[]{:S(2)}, u32[]{:S(2)}) collective-permute-start(f32[128,128]{1,0:T(8,128)S(1)} %add.15), channel_id=1, source_target_pairs={{0,2},{1,3},{2,0},{3,1},{4,6},{5,7},{6,4},{7,5},{8,10},{9,11},{10,... | collective-permute-start | bytes 196616 | tf_op jit(solution)/shard_map/ppermute | solution.py:24
  45.9 6.8 %collective-permute-start.16 = (f32[128,128]{1,0:T(8,128)S(1)}, f32[128,128]{1,0:T(8,128)S(1)}, u32[]{:S(2)}, u32[]{:S(2)}) collective-permute-start(f32[128,128]{1,0:T(8,128)S(1)} %add.16), channel_id=1, source_target_pairs={{0,4},{1,5},{2,6},{3,7},{4,0},{5,1},{6,2},{7,3},{8,12},{9,13},{10,... | collective-permute-start | bytes 196616 | tf_op jit(solution)/shard_map/ppermute | solution.py:24
  49.8 12.4 %collective-permute-start.20 = (bf16[1024,128]{1,0:T(8,128)(2,1)S(1)}, bf16[1024,128]{1,0:T(8,128)(2,1)S(1)}, u32[]{:S(2)}, u32[]{:S(2)}) collective-permute-start(bf16[1024,128]{1,0:T(8,128)(2,1)S(1)} %get-tuple-element.23), channel_id=1, source_target_pairs={{0,16},{8,24},{16,0},{24,8},{1,17},{9,25},{17,1},{25,9},{2,18},{10... | collective-permute-start | bytes 786440 | tf_op jit(solution)/shard_map/ppermute | solution.py:24
  52.7 5.0 %collective-permute-start.17 = (f32[128,128]{1,0:T(8,128)S(1)}, f32[128,128]{1,0:T(8,128)S(1)}, u32[]{:S(2)}, u32[]{:S(2)}) collective-permute-start(f32[128,128]{1,0:T(8,128)S(1)} %add.17), channel_id=1, source_target_pairs={{0,8},{8,0},{16,24},{24,16},{1,9},{9,1},{17,25},{25,17},{2,10},{10... | collective-permute-start | bytes 196616 | tf_op jit(solution)/shard_map/ppermute | solution.py:24
  54.0 10.6 %collective-permute-start.21 = (bf16[1024,128]{1,0:T(8,128)(2,1)S(1)}, bf16[1024,128]{1,0:T(8,128)(2,1)S(1)}, u32[]{:S(2)}, u32[]{:S(2)}) collective-permute-start(bf16[1024,128]{1,0:T(8,128)(2,1)S(1)} %get-tuple-element.24), channel_id=1, source_target_pairs={{0,24},{8,16},{16,8},{24,0},{1,25},{9,17},{17,9},{25,1},{2,26},{10... | collective-permute-start | bytes 786440 | tf_op jit(solution)/shard_map/ppermute | solution.py:24
  55.3 12.3 %collective-permute-start.4 = (bf16[1024,128]{1,0:T(8,128)(2,1)S(1)}, bf16[1024,128]{1,0:T(8,128)(2,1)S(1)}, u32[]{:S(2)}, u32[]{:S(2)}) collective-permute-start(bf16[1024,128]{1,0:T(8,128)(2,1)S(1)} %get-tuple-element.17), channel_id=1, source_target_pairs={{0,2},{1,3},{2,0},{3,1},{4,6},{5,7},{6,4},{7,5},{8,10},{9,11},{10,... | collective-permute-start | bytes 786440 | tf_op jit(solution)/shard_map/ppermute | solution.py:24
  57.7 20.1 %collective-permute-start.5 = (bf16[1024,128]{1,0:T(8,128)(2,1)S(1)}, bf16[1024,128]{1,0:T(8,128)(2,1)S(1)}, u32[]{:S(2)}, u32[]{:S(2)}) collective-permute-start(bf16[1024,128]{1,0:T(8,128)(2,1)S(1)} %get-tuple-element.18), channel_id=1, source_target_pairs={{0,4},{1,5},{2,6},{3,7},{4,0},{5,1},{6,2},{7,3},{8,12},{9,13},{10,... | collective-permute-start | bytes 786440 | tf_op jit(solution)/shard_map/ppermute | solution.py:24
  60.0 17.9 %collective-permute-start.6 = (bf16[1024,128]{1,0:T(8,128)(2,1)S(1)}, bf16[1024,128]{1,0:T(8,128)(2,1)S(1)}, u32[]{:S(2)}, u32[]{:S(2)}) collective-permute-start(bf16[1024,128]{1,0:T(8,128)(2,1)S(1)} %get-tuple-element.19), channel_id=1, source_target_pairs={{0,6},{1,7},{2,4},{3,5},{4,2},{5,3},{6,0},{7,1},{8,14},{9,15},{10,... | collective-permute-start | bytes 786440 | tf_op jit(solution)/shard_map/ppermute | solution.py:24
  62.2 4.7 %collective-permute-start.18 = (f32[128,128]{1,0:T(8,128)S(1)}, f32[128,128]{1,0:T(8,128)S(1)}, u32[]{:S(2)}, u32[]{:S(2)}) collective-permute-start(f32[128,128]{1,0:T(8,128)S(1)} %add.18), channel_id=1, source_target_pairs={{0,16},{8,24},{16,0},{24,8},{1,17},{9,25},{17,1},{25,9},{2,18},{10... | collective-permute-start | bytes 196616 | tf_op jit(solution)/shard_map/ppermute | solution.py:24

commit v3 on v2

--- a/solution.py
+++ b/solution.py
@@ -32,6 +32,10 @@
     return pl.CostEstimate(flops=flops, bytes_accessed=moved, transcendentals=0)
 
 
+def spot(k, count):
+    return 0 if count == 1 else (k % 2) * (count // 2) + spot(k // 2, count // 2)
+
+
 def load_kernel(count_ref, tiles, held, sems):
     chunk = held.shape[0] // sems.shape[0]
     chunks = pl.cdiv(count_ref[0, 0], chunk)
@@ -59,8 +63,7 @@
 
 
 def forward_kernel(n_shards, count_ref, rows_ref, cols_ref, tiles, *refs):
-    shards, (keep, send) = refs[:n_shards], refs[n_shards : n_shards + 2]
-    panel, acc = refs[n_shards + 2 :]
+    shards, (*outs, panel, acc) = refs[:n_shards], refs[n_shards:]
     slots, tile = tiles.shape[:2]
     own = shards[0].shape[0]
     dump = acc.shape[0] - 1
@@ -80,21 +83,22 @@
 
     for_slots(live, slots, work)
     per = own // tile
-    for k in range(keep.shape[0] // own):
+    half = outs[0].shape[0] // own
+    for k in range(2 * half):
         base = (line ^ k) * CORES
+        part, place = divmod(spot(k, 2 * half), half)
         for b in range(per):
-            span = pl.ds(k * own + b * tile, tile)
-            keep[span, :] = acc[(base + core) * per + b].astype(BF16)
-            send[span, :] = acc[(base + 1 - core) * per + b].astype(BF16)
-
-
-def backward_kernel(n_rows, n_lines, count_ref, rows_ref, cols_ref, tiles, scale, *refs):
+            span = pl.ds(place * own + b * tile, tile)
+            outs[part][span, :] = acc[(base + core) * per + b].astype(BF16)
+            span = pl.ds(b * tile, tile)
+            outs[2 + spot(k, 2 * half)][span, :] = acc[(base + 1 - core) * per + b].astype(BF16)
+
+
+def backward_kernel(n_rows, n_lines, count_ref, rows_ref, cols_ref, tiles, *refs):
     n_cots = n_lines * CORES
-    hids, cots, refs = refs[:n_rows], refs[n_rows : n_rows + n_cots], refs[n_rows + n_cots :]
-    outs, weight_term, refs = refs[:n_rows], refs[n_rows], refs[n_rows + 1 :]
-    turned, acc = refs
+    cots, outs, (turned, acc) = refs[:n_cots], refs[n_cots:-2], refs[-2:]
     slots, tile = tiles.shape[:2]
-    own = hids[0].shape[0]
+    own = cots[0].shape[0]
     per = own // tile
     dump = acc.shape[0] - 1
     live = count_ref[0, 0]
@@ -113,21 +117,34 @@
         acc[c] += jnp.dot(turned[r], tiles[s], preferred_element_type=F32)
 
     for_slots(live, slots, work)
-    total = jnp.zeros(weight_term.shape, F32)
     for k in range(n_rows):
         for b in range(per):
-            span = pl.ds(b * tile, tile)
-            part = acc[(row ^ k) * per + b]
-            total += jnp.dot(part.astype(BF16), hids[k][span, :], preferred_element_type=F32)
-            outs[k][span, :] = part.T.astype(BF16)
-    weight_term[...] = total.T * scale[0]
-
-
-def pair_kernel(keep, got, *outs):
-    own = outs[0].shape[0]
-    for k, out in enumerate(outs):
-        span = pl.ds(k * own, own)
-        out[...] = (keep[span, :].astype(F32) + got[span, :].astype(F32)).astype(BF16)
+            outs[k][b * tile : (b + 1) * tile, :] = acc[(row ^ k) * per + b].T.astype(BF16)
+
+
+def weight_kernel(scale, stay, away, *refs):
+    *cots, out = refs
+    own = cots[0].shape[0]
+    total = jnp.zeros(out.shape, F32)
+    for k, cot in enumerate(cots):
+        side, place = divmod(spot(k, len(cots)), len(cots) // 2)
+        part = (stay, away)[side][place * own : (place + 1) * own, :]
+        total += lax.dot_general(
+            part, cot[...], (((0,), (0,)), ((), ())), preferred_element_type=F32
+        )
+    out[...] = total * scale[0]
+
+
+def merge_kernel(keep, *refs):
+    *got, out = refs
+    for k, part in enumerate(got):
+        span = pl.ds(k * part.shape[0], part.shape[0])
+        out[span, :] = (keep[span, :].astype(F32) + part[...].astype(F32)).astype(BF16)
+
+
+def add_kernel(start, left, right, out):
+    span = pl.ds(start, out.shape[0])
+    out[...] = (left[span, :].astype(F32) + right[span, :].astype(F32)).astype(BF16)
 
 
 def summed(parts):
@@ -137,15 +154,22 @@
     return total.astype(BF16)
 
 
-def out_kernel(weight, *refs):
-    refs[-1][0] = jnp.dot(summed(refs[:-1]), weight[...], preferred_element_type=F32).astype(BF16)
-
-
-def grad_kernel(weight, mask, *refs):
-    turned = lax.dot_general(
-        summed(refs[:-1]), weight[...], (((1,), (1,)), ((), ())), preferred_element_type=F32
+def finish_kernel(n_rows, weight, mask, stay, got, *refs):
+    backs, terms = refs[:n_rows], refs[n_rows:-3]
+    out_pre, weight_grad, input_grad = refs[-3:]
+    weights = weight[...]
+    out_pre[0] = jnp.dot(summed((stay, got)), weights, preferred_element_type=F32).astype(BF16)
+    weight_grad[...] = tree([term[...] for term in terms])
+    grads = lax.dot_general(
+        summed(backs), weights, (((1,), (1,)), ((), ())), preferred_element_type=F32
     )
-    refs[-1][0] = (turned * mask[0].astype(F32)).astype(BF16)
+    input_grad[0] = (grads * mask[0].astype(F32)).astype(BF16)
+
+
+def tree(terms):
+    while len(terms) > 1:
+        terms = [a + b for a, b in zip(terms[::2], terms[1::2])]
+    return terms[0]
 
 
 def body(features, relu_mask, tiles, tile_rows, tile_cols, tile_count, weight, cotangent):
@@ -175,12 +199,12 @@
         name="load_tiles",
     )(tile_count, tiles)
 
-    half = jax.ShapeDtypeStruct((n_lines * own, width), BF16)
-    keep, send = pl.pallas_call(
+    half = jax.ShapeDtypeStruct((n_lines * own // 2, width), BF16)
+    keep_stay, keep_away, *send = pl.pallas_call(
         functools.partial(forward_kernel, n_rows),
-        out_shape=(half, half),
+        out_shape=(half,) * 2 + (block,) * n_lines,
         in_specs=[SMEM] * 3 + [VMEM] * (1 + n_rows),
-        out_specs=(VMEM, VMEM),
+        out_specs=(VMEM,) * (2 + n_lines),
         scratch_shapes=[
             pltpu.VMEM((n_rows * own, width), BF16),
             pltpu.VMEM((row_blocks + 1, tile, width), F32),
@@ -189,31 +213,48 @@
         cost_estimate=cost(work, 2 * tiles.size),
         name="forward_tiles",
     )(*ids, held, *hids)
-    got = swap(send, "col", 1)
-    pairs = pl.pallas_call(
-        pair_kernel,
-        out_shape=(block,) * n_lines,
-        in_specs=[VMEM] * 2,
-        out_specs=(VMEM,) * n_lines,
-        compiler_params=room(8),
-        name="pair_sum",
-    )(keep, got)
-    parts = [pairs[0]] + [swap(pairs[k], "col", CORES * k) for k in range(1, n_lines)]
-    out_pre = pl.pallas_call(
-        out_kernel,
-        out_shape=jax.ShapeDtypeStruct((1, own, width), BF16),
-        in_specs=[VMEM] * (1 + n_lines),
+
+    def merge(keep, got):
+        return pl.pallas_call(
+            merge_kernel,
+            out_shape=half,
+            in_specs=[VMEM] * (1 + len(got)),
+            out_specs=VMEM,
+            compiler_params=room(8),
+            name="merge_parts",
+        )(keep, *got)
+
+    def add(left, right, start, count):
+        return pl.pallas_call(
+            functools.partial(add_kernel, start * own),
+            out_shape=jax.ShapeDtypeStruct((count * own, width), BF16),
+            in_specs=[VMEM] * 2,
+            out_specs=VMEM,
+            compiler_params=room(8),
+            name="add_parts",
+        )(left, right)
+
+    pairs = [swap(part, "col", 1) for part in send]
+    got_stay, got_away = pairs[: n_lines // 2], pairs[n_lines // 2 :]
+    away = merge(keep_away, got_away)
+    got_stay, cots = lax.optimization_barrier((got_stay, cots))
+    stay = merge(keep_stay, got_stay)
+    got = swap(away, "col", CORES)
+    scale = 1.0 / jnp.sqrt(jnp.full((1,), own * n_rows * n_cols, F32))
+    weight_term = pl.pallas_call(
+        weight_kernel,
+        out_shape=jax.ShapeDtypeStruct((width, width), F32),
+        in_specs=[SMEM] + [VMEM] * (2 + n_lines),
         out_specs=VMEM,
         compiler_params=room(8),
-        name="out_pre",
-    )(weight, *parts)
-
-    scale = 1.0 / jnp.sqrt(jnp.full((1,), own * n_rows * n_cols, F32))
-    *backs, weight_term = pl.pallas_call(
+        name="weight_term",
+    )(scale, stay, away, *cots[::CORES])
+
+    backs = pl.pallas_call(
         functools.partial(backward_kernel, n_rows, n_lines),
-        out_shape=(block,) * n_rows + (jax.ShapeDtypeStruct((width, width), F32),),
-        in_specs=[SMEM] * 3 + [VMEM] + [SMEM] + [VMEM] * (n_rows + n_cols),
-        out_specs=(VMEM,) * (n_rows + 1),
+        out_shape=(block,) * n_rows,
+        in_specs=[SMEM] * 3 + [VMEM] * (1 + n_cols),
+        out_specs=(VMEM,) * n_rows,
         scratch_shapes=[
             pltpu.VMEM((row_blocks, width, tile), BF16),
             pltpu.VMEM((col_blocks + 1, width, tile), F32),
@@ -221,21 +262,29 @@
         compiler_params=room(WORK),
         cost_estimate=cost(work, 2 * tiles.size),
         name="backward_tiles",
-    )(*ids, held, scale, *hids, *cots)
+    )(*ids, held, *cots)
+    weight_term = weight_term + swap(weight_term, "col", 1)
+    terms = [weight_term] + [swap(weight_term, "row", k) for k in range(1, n_rows)]
+    backs, terms, got = lax.optimization_barrier((backs, terms, got))
+    weight_term = tree(terms)
+    bit, count = 1, n_lines // 2
+    while count > 1:
+        count, bit = count // 2, 2 * bit
+        away = swap(add(stay, got, count, count), "col", CORES * bit)
+        stay, got = add(stay, got, 0, count), away
     backs = [backs[0]] + [swap(backs[k], "row", k) for k in range(1, n_rows)]
-    input_grad = pl.pallas_call(
-        grad_kernel,
-        out_shape=jax.ShapeDtypeStruct((1, own, width), BF16),
-        in_specs=[VMEM] * (2 + n_rows),
-        out_specs=VMEM,
+    for b in range(n_lines.bit_length() - 2):
+        weight_term = weight_term + swap(weight_term, "col", CORES << b)
+    terms = [weight_term, swap(weight_term, "col", n_cols // 2)]
+    block = jax.ShapeDtypeStruct((1, own, width), BF16)
+    return pl.pallas_call(
+        functools.partial(finish_kernel, n_rows),
+        out_shape=(block, jax.ShapeDtypeStruct((width, width), F32), block),
+        in_specs=[VMEM] * (4 + n_rows + len(terms)),
+        out_specs=(VMEM,) * 3,
         compiler_params=room(8),
-        name="input_grad",
-    )(weight, relu_mask, *backs)
-
-    for axis, size in (("col", n_cols), ("row", n_rows)):
-        for bit in range(size.bit_length() - 1):
-            weight_term = weight_term + swap(weight_term, axis, 1 << bit)
-    return (out_pre, weight_term, input_grad)
+        name="finish",
+    )(weight, relu_mask, stay, got, *backs, *terms)
 
 
 def solution(mesh):

time: 79.7 us -> 65.9 us (0.83)
  waiting for transfers between devices: 22.6 us -> 14.2 us
  starting transfers between devices: 26.7 us -> 22.5 us
    ppermute x22 -> x25, waiting for transfers between devices: 22.6 us -> 14.2 us  [swap(): return lax.ppermute(value, axis, [(i, i ^ step) for i in range(size)])]
    ppermute x22 -> x25, starting transfers between devices: 26.7 us -> 22.5 us  [swap(): return lax.ppermute(value, axis, [(i, i ^ step) for i in range(size)])]
    pallas_call x3 -> x6, Pallas kernels: 2.18 us -> 1.97 us  [the longest x1 1.11 us: body(): pl.pallas_call(functools.partial(finish_kernel, n_rows), out_shape=(block...]
  transfers between devices with their start and end apart: 22 -> 25, of which waited for: 12 -> 8; matrix products, arithmetic and copies ran while one was open for 1% -> 0% of each run, Pallas kernels for 32% -> 38%
where the time goes in v3:
time: 65.9 us; the launch traced here: 65.3 us
  Pallas kernels  25.8 us (39%)
  starting transfers between devices  22.5 us (34%)
  waiting for transfers between devices  14.2 us (22%)
  between operations  1.55 us (2%)
  other arithmetic  1.2 us (2%)
    ppermute x25, starting transfers between devices, swap(): return lax.ppermute(value, axis, [(i, i ^ step) for i in range(size)])  22.5 us
    ppermute x25, waiting for transfers between devices, swap(): return lax.ppermute(value, axis, [(i, i ^ step) for i in range(size)])  14.2 us
    pallas_call x1, Pallas kernels, body(): pl.pallas_call(functools.partial(forward_kernel, n_rows), out_shape=(half...  8.73 us
    pallas_call x1, Pallas kernels, body(): pl.pallas_call(load_kernel, out_shape=jax.ShapeDtypeStruct((slots, tile,...  8.15 us
    pallas_call x1, Pallas kernels, body(): pl.pallas_call(functools.partial(backward_kernel, n_rows, n_lines), out_s...  6.94 us
  transfers between devices with their start and end apart: 25, of which 8 were waited for; matrix products, arithmetic and copies ran while one was open for 0% of the time, Pallas kernels for 38%

profile of v3, /device:TPU:0, one launch (start us, length us, event | category | flops | bytes accessed | tf_op | source)
XLA Modules:
  0.0 65.3 jit_solution(17349854547781279595)
XLA Ops:
  0.6 1.2 %multiply_bitcast_fusion.refs_0_ = bf16[1024,128]{1,0:T(8,128)(2,1)S(1)} fusion(bf16[1,1024,128]{2,1,0:T(8,128)(2,1)} %param.8, s32[1,1024,128]{2,1,0:T(8,128)} %mask.1), kind=kLoop, calls=%fused_computation | loop fusion | flops 262144 | bytes 1048576 | tf_op jit(solution)/shard_map/mul | solution.py:188
  1.8 3.0 %collective-permute-start = (bf16[1024,128]{1,0:T(8,128)(2,1)S(1)}, bf16[1024,128]{1,0:T(8,128)(2,1)S(1)}, u32[]{:S(2)}, u32[]{:S(2)}) collective-permute-start(bf16[1024,128]{1,0:T(8,128)(2,1)S(1)} %multiply_bitcast_fusion.refs_0_), channel_id=1, source_target_pairs={{0,8},{8,0},{16,24},{24,16},{1,9},{9,1},{17,25},{25,17},{2,10},{10... | collective-permute-start | bytes 786440 | tf_op jit(solution)/shard_map/ppermute | solution.py:24
  4.8 1.5 %collective-permute-start.1 = (bf16[1024,128]{1,0:T(8,128)(2,1)S(1)}, bf16[1024,128]{1,0:T(8,128)(2,1)S(1)}, u32[]{:S(2)}, u32[]{:S(2)}) collective-permute-start(bf16[1024,128]{1,0:T(8,128)(2,1)S(1)} %multiply_bitcast_fusion.refs_0_), channel_id=1, source_target_pairs={{0,16},{8,24},{16,0},{24,8},{1,17},{9,25},{17,1},{25,9},{2,18},{10... | collective-permute-start | bytes 786440 | tf_op jit(solution)/shard_map/ppermute | solution.py:24
  6.3 4.1 %collective-permute-start.10 = (bf16[1024,128]{1,0:T(8,128)(2,1)}, bf16[1024,128]{1,0:T(8,128)(2,1)S(1)}, u32[]{:S(2)}, u32[]{:S(2)}) collective-permute-start(bf16[1024,128]{1,0:T(8,128)(2,1)} %bitcast.3), channel_id=1, source_target_pairs={{0,6},{1,7},{2,4},{3,5},{4,2},{5,3},{6,0},{7,1},{8,14},{9,15},{10,... | collective-permute-start | bytes 786440 | tf_op jit(solution)/shard_map/ppermute | solution.py:24
  11.1 8.2 %load_tiles.1.tiles = bf16[184,256,256]{2,1,0:T(8,128)(2,1)S(1)} custom-call(s32[1,1]{1,0:T(1,128)S(6)} %copy.11.count_ref, bf16[1,1,184,256,256]{4,3,2,1,0:T(8,128)(2,1)} %tiles.1), custom_call_target="tpu_custom_call" | custom-call | bytes 24117248 | tf_op jit(solution)/shard_map/load_tiles/pallas_call | solution.py:191
  19.5 8.7 %forward_tiles.1 = (bf16[2048,128]{1,0:T(8,128)(2,1)S(1)}, bf16[2048,128]{1,0:T(8,128)(2,1)S(1)}, bf16[1024,128]{1,0:T(8,128)(2,1)S(1)}, bf16[1024,128]{1,0:T(8,...) custom-call(s32[1,1]{1,0:T(1,128)S(6)} %copy.11.count_ref, s32[1,1,184]{2,1,0:T(1,128)S(1)} %copy-done.3, ...), custom_call_target="tpu_custom_call" | custom-call | flops 3087007744 | bytes 24117248 | tf_op jit(solution)/shard_map/forward_tiles/pallas_call | solution.py:203
  28.3 0.5 collective-permute-start.13
  28.9 3.2 %collective-permute-done.8.refs_4_.refs_2_ = bf16[1024,128]{1,0:T(8,128)(2,1)S(1)} collective-permute-done((bf16[1024,128]{1,0:T(8,128)(2,1)S(1)}, bf16[1024,128]{1,0:T(8,128)(2,1)S(1)}, u32[]{:S(2)}, u32[]{:S(2)}) %collective-permute-start.8) | collective-permute-done | bytes 262176 | tf_op jit(solution)/shard_map/ppermute | solution.py:24
  32.1 0.5 collective-permute-start.11
  32.7 0.4 collective-permute-start.9
  33.1 0.1 merge_parts.3.away
  33.3 0.3 collective-permute-done.4.refs_1_
  33.6 0.4 collective-permute-done.11.refs_7_
  34.0 0.4 collective-permute-done.7.refs_3_
  34.4 0.4 collective-permute-done.9.refs_5_
  34.7 0.1 merge_parts.2.stay.left
  34.9 0.5 weight_term.1
  35.4 0.2 collective-permute-start.14
  35.6 1.1 %collective-permute-done.14 = f32[128,128]{1,0:T(8,128)S(1)} collective-permute-done((f32[128,128]{1,0:T(8,128)S(1)}, f32[128,128]{1,0:T(8,128)S(1)}, u32[]{:S(2)}, u32[]{:S(2)}) %collective-permute-start.14) | collective-permute-done | bytes 65568 | tf_op jit(solution)/shard_map/ppermute | solution.py:24
  36.7 1.6 %collective-permute-start.15 = (f32[128,128]{1,0:T(8,128)S(1)}, f32[128,128]{1,0:T(8,128)S(1)}, u32[]{:S(2)}, u32[]{:S(2)}) collective-permute-start(f32[128,128]{1,0:T(8,128)S(1)} %add.15), channel_id=1, source_target_pairs={{0,8},{8,0},{16,24},{24,16},{1,9},{9,1},{17,25},{25,17},{2,10},{10... | collective-permute-start | bytes 196616 | tf_op jit(solution)/shard_map/ppermute | solution.py:24
  38.2 1.5 %collective-permute-start.16 = (f32[128,128]{1,0:T(8,128)S(1)}, f32[128,128]{1,0:T(8,128)S(1)}, u32[]{:S(2)}, u32[]{:S(2)}) collective-permute-start(f32[128,128]{1,0:T(8,128)S(1)} %add.15), channel_id=1, source_target_pairs={{0,16},{8,24},{16,0},{24,8},{1,17},{9,25},{17,1},{25,9},{2,18},{10... | collective-permute-start | bytes 196616 | tf_op jit(solution)/shard_map/ppermute | solution.py:24
  39.8 0.7 %collective-permute-start.17 = (f32[128,128]{1,0:T(8,128)S(1)}, f32[128,128]{1,0:T(8,128)S(1)}, u32[]{:S(2)}, u32[]{:S(2)}) collective-permute-start(f32[128,128]{1,0:T(8,128)S(1)} %add.15), channel_id=1, source_target_pairs={{0,24},{8,16},{16,8},{24,0},{1,25},{9,17},{17,9},{25,1},{2,26},{10... | collective-permute-start | bytes 196616 | tf_op jit(solution)/shard_map/ppermute | solution.py:24
  40.5 6.9 %backward_tiles.1 = (bf16[1024,128]{1,0:T(8,128)(2,1)S(1)}, bf16[1024,128]{1,0:T(8,128)(2,1)S(1)}, bf16[1024,128]{1,0:T(8,128)(2,1)S(1)}, bf16[1024,128]{1,0:T(8,128)(2,1)S(1)}) custom-call(s32[1,1]{1,0:T(1,128)S(6)} %copy.11.count_ref, s32[1,1,184]{2,1,0:T(1,128)S(1)} %copy-done.3, s32[1,1,184]{2,1,0:T(1,128)S(1)} %copy-done.4, ...), custom_call_target="tpu_custom_call" | custom-call | flops 3087007744 | bytes 24117248 | tf_op jit(solution)/shard_map/backward_tiles/pallas_call | solution.py:253
  47.6 1.1 %collective-permute-start.19 = (bf16[1024,128]{1,0:T(8,128)(2,1)S(1)}, bf16[1024,128]{1,0:T(8,128)(2,1)S(1)}, u32[]{:S(2)}, u32[]{:S(2)}) collective-permute-start(bf16[1024,128]{1,0:T(8,128)(2,1)S(1)} %add_parts.3), channel_id=1, source_target_pairs={{0,4},{1,5},{2,6},{3,7},{4,0},{5,1},{6,2},{7,3},{8,12},{9,13},{10,... | collective-permute-start | bytes 786440 | tf_op jit(solution)/shard_map/ppermute | solution.py:24
  48.6 1.5 %collective-permute-start.20 = (bf16[1024,128]{1,0:T(8,128)(2,1)S(1)}, bf16[1024,128]{1,0:T(8,128)(2,1)S(1)}, u32[]{:S(2)}, u32[]{:S(2)}) collective-permute-start(bf16[1024,128]{1,0:T(8,128)(2,1)S(1)} %get-tuple-element.54), channel_id=1, source_target_pairs={{0,8},{8,0},{16,24},{24,16},{1,9},{9,1},{17,25},{25,17},{2,10},{10... | collective-permute-start | bytes 786440 | tf_op jit(solution)/shard_map/ppermute | solution.py:24
  50.1 1.5 %collective-permute-start.21 = (bf16[1024,128]{1,0:T(8,128)(2,1)S(1)}, bf16[1024,128]{1,0:T(8,128)(2,1)S(1)}, u32[]{:S(2)}, u32[]{:S(2)}) collective-permute-start(bf16[1024,128]{1,0:T(8,128)(2,1)S(1)} %get-tuple-element.55), channel_id=1, source_target_pairs={{0,16},{8,24},{16,0},{24,8},{1,17},{9,25},{17,1},{25,9},{2,18},{10... | collective-permute-start | bytes 786440 | tf_op jit(solution)/shard_map/ppermute | solution.py:24
  51.7 0.5 collective-permute-start.22
  52.1 1.8 %collective-permute-start.23 = (f32[128,128]{1,0:T(8,128)S(1)}, f32[128,128]{1,0:T(8,128)S(1)}, u32[]{:S(2)}, u32[]{:S(2)}) collective-permute-start(f32[128,128]{1,0:T(8,128)S(1)} %add_add_fusion), channel_id=1, source_target_pairs={{0,2},{1,3},{2,0},{3,1},{4,6},{5,7},{6,4},{7,5},{8,10},{9,11},{10,... | collective-permute-start | bytes 196616 | tf_op jit(solution)/shard_map/ppermute | solution.py:24
  54.0 2.9 %collective-permute-done.23 = f32[128,128]{1,0:T(8,128)S(1)} collective-permute-done((f32[128,128]{1,0:T(8,128)S(1)}, f32[128,128]{1,0:T(8,128)S(1)}, u32[]{:S(2)}, u32[]{:S(2)}) %collective-permute-start.23) | collective-permute-done | bytes 65568 | tf_op jit(solution)/shard_map/ppermute | solution.py:24
  56.8 1.7 %collective-permute-start.24 = (f32[128,128]{1,0:T(8,128)S(1)}, f32[128,128]{1,0:T(8,128)S(1)}, u32[]{:S(2)}, u32[]{:S(2)}) collective-permute-start(f32[128,128]{1,0:T(8,128)S(1)} %add.19.refs_4_), channel_id=1, source_target_pairs={{0,4},{1,5},{2,6},{3,7},{4,0},{5,1},{6,2},{7,3},{8,12},{9,13},{10,... | collective-permute-start | bytes 196616 | tf_op jit(solution)/shard_map/ppermute | solution.py:24
  58.6 5.5 %collective-permute-done.24.refs_5_ = f32[128,128]{1,0:T(8,128)S(1)} collective-permute-done((f32[128,128]{1,0:T(8,128)S(1)}, f32[128,128]{1,0:T(8,128)S(1)}, u32[]{:S(2)}, u32[]{:S(2)}) %collective-permute-start.24) | collective-permute-done | bytes 65568 | tf_op jit(solution)/shard_map/ppermute | solution.py:24
  64.1 1.1 %finish.1 = (bf16[1,1024,128]{2,1,0:T(8,128)(2,1)}, f32[128,128]{1,0:T(8,128)}, bf16[1,1024,128]{2,1,0:T(8,128)(2,1)}) custom-call(bf16[128,128]{1,0:T(8,128)(2,1)S(1)} %copy-done.2, s32[1,1024,128]{2,1,0:T(8,128)S(1)} %copy-done, bf16[1024,128]{1,0:T(8,128)(2,1)S(1)} %add_parts.2.stay, bf16[1024,128]{1,0:T(8,128)(2,1)S(1)} %collective-permute-done.19.got, ...), custom_call_target="tpu_custom_call" | custom-call | tf_op jit(solution)/shard_map/finish/pallas_call | solution.py:280
  (41 shorter events, 0.7 us)
Async XLA Ops:
  1.8 17.5 %collective-permute-start = (bf16[1024,128]{1,0:T(8,128)(2,1)S(1)}, bf16[1024,128]{1,0:T(8,128)(2,1)S(1)}, u32[]{:S(2)}, u32[]{:S(2)}) collective-permute-start(bf16[1024,128]{1,0:T(8,128)(2,1)S(1)} %multiply_bitcast_fusion.refs_0_), channel_id=1, source_target_pairs={{0,8},{8,0},{16,24},{24,16},{1,9},{9,1},{17,25},{25,17},{2,10},{10... | collective-permute-start | bytes 786440 | tf_op jit(solution)/shard_map/ppermute | solution.py:24
  4.8 14.6 %collective-permute-start.1 = (bf16[1024,128]{1,0:T(8,128)(2,1)S(1)}, bf16[1024,128]{1,0:T(8,128)(2,1)S(1)}, u32[]{:S(2)}, u32[]{:S(2)}) collective-permute-start(bf16[1024,128]{1,0:T(8,128)(2,1)S(1)} %multiply_bitcast_fusion.refs_0_), channel_id=1, source_target_pairs={{0,16},{8,24},{16,0},{24,8},{1,17},{9,25},{17,1},{25,9},{2,18},{10... | collective-permute-start | bytes 786440 | tf_op jit(solution)/shard_map/ppermute | solution.py:24
  6.3 13.1 %collective-permute-start.2 = (bf16[1024,128]{1,0:T(8,128)(2,1)S(1)}, bf16[1024,128]{1,0:T(8,128)(2,1)S(1)}, u32[]{:S(2)}, u32[]{:S(2)}) collective-permute-start(bf16[1024,128]{1,0:T(8,128)(2,1)S(1)} %multiply_bitcast_fusion.refs_0_), channel_id=1, source_target_pairs={{0,24},{8,16},{16,8},{24,0},{1,25},{9,17},{17,9},{25,1},{2,26},{10... | collective-permute-start | bytes 786440 | tf_op jit(solution)/shard_map/ppermute | solution.py:24
  6.3 22.0 %collective-permute-start.10 = (bf16[1024,128]{1,0:T(8,128)(2,1)}, bf16[1024,128]{1,0:T(8,128)(2,1)S(1)}, u32[]{:S(2)}, u32[]{:S(2)}) collective-permute-start(bf16[1024,128]{1,0:T(8,128)(2,1)} %bitcast.3), channel_id=1, source_target_pairs={{0,6},{1,7},{2,4},{3,5},{4,2},{5,3},{6,0},{7,1},{8,14},{9,15},{10,... | collective-permute-start | bytes 786440 | tf_op jit(solution)/shard_map/ppermute | solution.py:24
  10.4 18.4 %collective-permute-start.6 = (bf16[1024,128]{1,0:T(8,128)(2,1)}, bf16[1024,128]{1,0:T(8,128)(2,1)S(1)}, u32[]{:S(2)}, u32[]{:S(2)}) collective-permute-start(bf16[1024,128]{1,0:T(8,128)(2,1)} %bitcast.4), channel_id=1, source_target_pairs={{0,2},{1,3},{2,0},{3,1},{4,6},{5,7},{6,4},{7,5},{8,10},{9,11},{10,... | collective-permute-start | bytes 786440 | tf_op jit(solution)/shard_map/ppermute | solution.py:24
  11.1 8.2 %copy-start.1 = (bf16[1,1024,128]{2,1,0:T(8,128)(2,1)S(1)}, bf16[1,1024,128]{2,1,0:T(8,128)(2,1)}, u32[]{:S(2)}) copy-start(bf16[1,1024,128]{2,1,0:T(8,128)(2,1)} %param.15) | copy-start | bytes 786436
  11.1 8.4 %copy-start.3 = (s32[1,1,184]{2,1,0:T(1,128)S(1)}, s32[1,1,184]{2,1,0:T(1,128)}, u32[]{:S(2)}) copy-start(s32[1,1,184]{2,1,0:T(1,128)} %rows_ref.3) | copy-start | bytes 2212
  11.1 8.4 %copy-start.4 = (s32[1,1,184]{2,1,0:T(1,128)S(1)}, s32[1,1,184]{2,1,0:T(1,128)}, u32[]{:S(2)}) copy-start(s32[1,1,184]{2,1,0:T(1,128)} %cols_ref.3) | copy-start | bytes 2212
  19.2 44.9 %copy-start = (s32[1,1024,128]{2,1,0:T(8,128)S(1)}, s32[1,1024,128]{2,1,0:T(8,128)}, u32[]{:S(2)}) copy-start(s32[1,1024,128]{2,1,0:T(8,128)} %mask.1) | copy-start | bytes 1572868
  19.3 44.9 %copy-start.2 = (bf16[128,128]{1,0:T(8,128)(2,1)S(1)}, bf16[128,128]{1,0:T(8,128)(2,1)}, u32[]{:S(2)}) copy-start(bf16[128,128]{1,0:T(8,128)(2,1)} %weight.1) | copy-start | bytes 98308
  19.3 12.8 %collective-permute-start.8 = (bf16[1024,128]{1,0:T(8,128)(2,1)S(1)}, bf16[1024,128]{1,0:T(8,128)(2,1)S(1)}, u32[]{:S(2)}, u32[]{:S(2)}) collective-permute-start(bf16[1024,128]{1,0:T(8,128)(2,1)S(1)} %bitcast.5), channel_id=1, source_target_pairs={{0,4},{1,5},{2,6},{3,7},{4,0},{5,1},{6,2},{7,3},{8,12},{9,13},{10,... | collective-permute-start | bytes 786440 | tf_op jit(solution)/shard_map/ppermute | solution.py:24
  19.4 12.7 %collective-permute-start.5 = (bf16[1024,128]{1,0:T(8,128)(2,1)S(1)}, bf16[1024,128]{1,0:T(8,128)(2,1)S(1)}, u32[]{:S(2)}, u32[]{:S(2)}) collective-permute-start(bf16[1024,128]{1,0:T(8,128)(2,1)S(1)} %bitcast.6), channel_id=1, source_target_pairs={{0,1},{1,0},{2,3},{3,2},{4,5},{5,4},{6,7},{7,6},{8,9},{9,8},{10,11... | collective-permute-start | bytes 786440 | tf_op jit(solution)/shard_map/ppermute | solution.py:24
  28.2 4.4 %collective-permute-start.12 = (bf16[1024,128]{1,0:T(8,128)(2,1)S(1)}, bf16[1024,128]{1,0:T(8,128)(2,1)S(1)}, u32[]{:S(2)}, u32[]{:S(2)}) collective-permute-start(bf16[1024,128]{1,0:T(8,128)(2,1)S(1)} %get-tuple-element.50), channel_id=1, source_target_pairs={{0,1},{1,0},{2,3},{3,2},{4,5},{5,4},{6,7},{7,6},{8,9},{9,8},{10,11... | collective-permute-start | bytes 786440 | tf_op jit(solution)/shard_map/ppermute | solution.py:24
  28.3 4.3 %collective-permute-start.13 = (bf16[1024,128]{1,0:T(8,128)(2,1)S(1)}, bf16[1024,128]{1,0:T(8,128)(2,1)S(1)}, u32[]{:S(2)}, u32[]{:S(2)}) collective-permute-start(bf16[1024,128]{1,0:T(8,128)(2,1)S(1)} %get-tuple-element.51), channel_id=1, source_target_pairs={{0,1},{1,0},{2,3},{3,2},{4,5},{5,4},{6,7},{7,6},{8,9},{9,8},{10,11... | collective-permute-start | bytes 786440 | tf_op jit(solution)/shard_map/ppermute | solution.py:24
  28.8 4.4 %collective-permute-start.3 = (bf16[1024,128]{1,0:T(8,128)(2,1)S(1)}, bf16[1024,128]{1,0:T(8,128)(2,1)S(1)}, u32[]{:S(2)}, u32[]{:S(2)}) collective-permute-start(bf16[1024,128]{1,0:T(8,128)(2,1)S(1)} %get-tuple-element.33), channel_id=1, source_target_pairs={{0,1},{1,0},{2,3},{3,2},{4,5},{5,4},{6,7},{7,6},{8,9},{9,8},{10,11... | collective-permute-start | bytes 786440 | tf_op jit(solution)/shard_map/ppermute | solution.py:24
  32.1 1.5 %collective-permute-start.4 = (bf16[1024,128]{1,0:T(8,128)(2,1)S(1)}, bf16[1024,128]{1,0:T(8,128)(2,1)S(1)}, u32[]{:S(2)}, u32[]{:S(2)}) collective-permute-start(bf16[1024,128]{1,0:T(8,128)(2,1)S(1)} %get-tuple-element.34), channel_id=1, source_target_pairs={{0,1},{1,0},{2,3},{3,2},{4,5},{5,4},{6,7},{7,6},{8,9},{9,8},{10,11... | collective-permute-start | bytes 786440 | tf_op jit(solution)/shard_map/ppermute | solution.py:24
  32.1 1.9 %collective-permute-start.11 = (bf16[1024,128]{1,0:T(8,128)(2,1)S(1)}, bf16[1024,128]{1,0:T(8,128)(2,1)S(1)}, u32[]{:S(2)}, u32[]{:S(2)}) collective-permute-start(bf16[1024,128]{1,0:T(8,128)(2,1)S(1)} %collective-permute-done.10.refs_6_.refs_3_), channel_id=1, source_target_pairs={{0,1},{1,0},{2,3},{3,2},{4,5},{5,4},{6,7},{7,6},{8,9},{9,8},{10,11... | collective-permute-start | bytes 786440 | tf_op jit(solution)/shard_map/ppermute | solution.py:24
  32.6 1.8 %collective-permute-start.7 = (bf16[1024,128]{1,0:T(8,128)(2,1)S(1)}, bf16[1024,128]{1,0:T(8,128)(2,1)S(1)}, u32[]{:S(2)}, u32[]{:S(2)}) collective-permute-start(bf16[1024,128]{1,0:T(8,128)(2,1)S(1)} %collective-permute-done.6.refs_2_.refs_1_), channel_id=1, source_target_pairs={{0,1},{1,0},{2,3},{3,2},{4,5},{5,4},{6,7},{7,6},{8,9},{9,8},{10,11... | collective-permute-start | bytes 786440 | tf_op jit(solution)/shard_map/ppermute | solution.py:24
  32.7 2.1 %collective-permute-start.9 = (bf16[1024,128]{1,0:T(8,128)(2,1)S(1)}, bf16[1024,128]{1,0:T(8,128)(2,1)S(1)}, u32[]{:S(2)}, u32[]{:S(2)}) collective-permute-start(bf16[1024,128]{1,0:T(8,128)(2,1)S(1)} %collective-permute-done.8.refs_4_.refs_2_), channel_id=1, source_target_pairs={{0,1},{1,0},{2,3},{3,2},{4,5},{5,4},{6,7},{7,6},{8,9},{9,8},{10,11... | collective-permute-start | bytes 786440 | tf_op jit(solution)/shard_map/ppermute | solution.py:24
  33.2 14.2 %collective-permute-start.18 = (bf16[2048,128]{1,0:T(8,128)(2,1)S(1)}, bf16[2048,128]{1,0:T(8,128)(2,1)S(1)}, u32[]{:S(2)}, u32[]{:S(2)}) collective-permute-start(bf16[2048,128]{1,0:T(8,128)(2,1)S(1)} %merge_parts.3.away), channel_id=1, source_target_pairs={{0,2},{1,3},{2,0},{3,1},{4,6},{5,7},{6,4},{7,5},{8,10},{9,11},{10,... | collective-permute-start | bytes 1572872 | tf_op jit(solution)/shard_map/ppermute | solution.py:24
  35.4 1.3 %collective-permute-start.14 = (f32[128,128]{1,0:T(8,128)S(1)}, f32[128,128]{1,0:T(8,128)S(1)}, u32[]{:S(2)}, u32[]{:S(2)}) collective-permute-start(f32[128,128]{1,0:T(8,128)S(1)} %weight_term.1), channel_id=1, source_target_pairs={{0,1},{1,0},{2,3},{3,2},{4,5},{5,4},{6,7},{7,6},{8,9},{9,8},{10,11... | collective-permute-start | bytes 196616 | tf_op jit(solution)/shard_map/ppermute | solution.py:24
  36.7 10.8 %collective-permute-start.15 = (f32[128,128]{1,0:T(8,128)S(1)}, f32[128,128]{1,0:T(8,128)S(1)}, u32[]{:S(2)}, u32[]{:S(2)}) collective-permute-start(f32[128,128]{1,0:T(8,128)S(1)} %add.15), channel_id=1, source_target_pairs={{0,8},{8,0},{16,24},{24,16},{1,9},{9,1},{17,25},{25,17},{2,10},{10... | collective-permute-start | bytes 196616 | tf_op jit(solution)/shard_map/ppermute | solution.py:24
  38.2 9.2 %collective-permute-start.16 = (f32[128,128]{1,0:T(8,128)S(1)}, f32[128,128]{1,0:T(8,128)S(1)}, u32[]{:S(2)}, u32[]{:S(2)}) collective-permute-start(f32[128,128]{1,0:T(8,128)S(1)} %add.15), channel_id=1, source_target_pairs={{0,16},{8,24},{16,0},{24,8},{1,17},{9,25},{17,1},{25,9},{2,18},{10... | collective-permute-start | bytes 196616 | tf_op jit(solution)/shard_map/ppermute | solution.py:24
  39.8 7.7 %collective-permute-start.17 = (f32[128,128]{1,0:T(8,128)S(1)}, f32[128,128]{1,0:T(8,128)S(1)}, u32[]{:S(2)}, u32[]{:S(2)}) collective-permute-start(f32[128,128]{1,0:T(8,128)S(1)} %add.15), channel_id=1, source_target_pairs={{0,24},{8,16},{16,8},{24,0},{1,25},{9,17},{17,9},{25,1},{2,26},{10... | collective-permute-start | bytes 196616 | tf_op jit(solution)/shard_map/ppermute | solution.py:24
  47.6 16.5 %collective-permute-start.19 = (bf16[1024,128]{1,0:T(8,128)(2,1)S(1)}, bf16[1024,128]{1,0:T(8,128)(2,1)S(1)}, u32[]{:S(2)}, u32[]{:S(2)}) collective-permute-start(bf16[1024,128]{1,0:T(8,128)(2,1)S(1)} %add_parts.3), channel_id=1, source_target_pairs={{0,4},{1,5},{2,6},{3,7},{4,0},{5,1},{6,2},{7,3},{8,12},{9,13},{10,... | collective-permute-start | bytes 786440 | tf_op jit(solution)/shard_map/ppermute | solution.py:24
  48.6 15.5 %collective-permute-start.20 = (bf16[1024,128]{1,0:T(8,128)(2,1)S(1)}, bf16[1024,128]{1,0:T(8,128)(2,1)S(1)}, u32[]{:S(2)}, u32[]{:S(2)}) collective-permute-start(bf16[1024,128]{1,0:T(8,128)(2,1)S(1)} %get-tuple-element.54), channel_id=1, source_target_pairs={{0,8},{8,0},{16,24},{24,16},{1,9},{9,1},{17,25},{25,17},{2,10},{10... | collective-permute-start | bytes 786440 | tf_op jit(solution)/shard_map/ppermute | solution.py:24
  50.1 14.0 %collective-permute-start.21 = (bf16[1024,128]{1,0:T(8,128)(2,1)S(1)}, bf16[1024,128]{1,0:T(8,128)(2,1)S(1)}, u32[]{:S(2)}, u32[]{:S(2)}) collective-permute-start(bf16[1024,128]{1,0:T(8,128)(2,1)S(1)} %get-tuple-element.55), channel_id=1, source_target_pairs={{0,16},{8,24},{16,0},{24,8},{1,17},{9,25},{17,1},{25,9},{2,18},{10... | collective-permute-start | bytes 786440 | tf_op jit(solution)/shard_map/ppermute | solution.py:24
  51.7 12.5 %collective-permute-start.22 = (bf16[1024,128]{1,0:T(8,128)(2,1)S(1)}, bf16[1024,128]{1,0:T(8,128)(2,1)S(1)}, u32[]{:S(2)}, u32[]{:S(2)}) collective-permute-start(bf16[1024,128]{1,0:T(8,128)(2,1)S(1)} %get-tuple-element.56), channel_id=1, source_target_pairs={{0,24},{8,16},{16,8},{24,0},{1,25},{9,17},{17,9},{25,1},{2,26},{10... | collective-permute-start | bytes 786440 | tf_op jit(solution)/shard_map/ppermute | solution.py:24
  52.1 4.7 %collective-permute-start.23 = (f32[128,128]{1,0:T(8,128)S(1)}, f32[128,128]{1,0:T(8,128)S(1)}, u32[]{:S(2)}, u32[]{:S(2)}) collective-permute-start(f32[128,128]{1,0:T(8,128)S(1)} %add_add_fusion), channel_id=1, source_target_pairs={{0,2},{1,3},{2,0},{3,1},{4,6},{5,7},{6,4},{7,5},{8,10},{9,11},{10,... | collective-permute-start | bytes 196616 | tf_op jit(solution)/shard_map/ppermute | solution.py:24
  56.8 7.3 %collective-permute-start.24 = (f32[128,128]{1,0:T(8,128)S(1)}, f32[128,128]{1,0:T(8,128)S(1)}, u32[]{:S(2)}, u32[]{:S(2)}) collective-permute-start(f32[128,128]{1,0:T(8,128)S(1)} %add.19.refs_4_), channel_id=1, source_target_pairs={{0,4},{1,5},{2,6},{3,7},{4,0},{5,1},{6,2},{7,3},{8,12},{9,13},{10,... | collective-permute-start | bytes 196616 | tf_op jit(solution)/shard_map/ppermute | solution.py:24

commit v4 on v3

--- a/solution.py
+++ b/solution.py
@@ -10,7 +10,7 @@
 
 CORES = 2
 MIB = 2**20
-UNROLL = 23
+UNROLL = 92
 WORK = 20
 F32 = jnp.float32
 BF16 = jnp.bfloat16
@@ -36,52 +36,73 @@
     return 0 if count == 1 else (k % 2) * (count // 2) + spot(k // 2, count // 2)
 
 
+def tile_copies(tiles, start, count, live):
+    chunk = math.gcd(count, 4)
+
+    def copy(held, sems, i):
+        source = tiles.at[0, 0, pl.ds(start + i * chunk, chunk)]
+        return pltpu.make_async_copy(source, held.at[pl.ds(i * chunk, chunk)], sems.at[i])
+
+    needed = jnp.minimum(pl.cdiv(jnp.maximum(live - start, 0), chunk), count // chunk)
+    return copy, needed
+
+
 def load_kernel(count_ref, tiles, held, sems):
-    chunk = held.shape[0] // sems.shape[0]
-    chunks = pl.cdiv(count_ref[0, 0], chunk)
-
-    def copy(i):
-        span = pl.ds(i * chunk, chunk)
-        return pltpu.make_async_copy(tiles.at[0, 0, span], held.at[span], sems.at[i])
-
-    @pl.loop(0, chunks)
-    def _(i):
-        copy(i).start()
-
-    @pl.loop(0, chunks)
-    def _(i):
-        copy(i).wait()
-
-
-def for_slots(live, slots, work):
-    unroll = math.gcd(slots, UNROLL)
-
-    @pl.loop(0, pl.cdiv(live, unroll))
+    copy, needed = tile_copies(tiles, 0, held.shape[0], count_ref[0, 0])
+
+    @pl.loop(0, needed)
+    def _(i):
+        copy(held, sems, i).start()
+
+    @pl.loop(0, needed)
+    def _(i):
+        copy(held, sems, i).wait()
+
+
+def for_slots(live, held, start, work):
+    count = held.shape[0]
+    unroll = math.gcd(count, UNROLL)
+    passes = jnp.minimum(pl.cdiv(jnp.maximum(live - start, 0), unroll), count // unroll)
+
+    @pl.loop(0, passes)
     def _(i):
         for j in range(unroll):
-            work(i * unroll + j)
-
-
-def forward_kernel(n_shards, count_ref, rows_ref, cols_ref, tiles, *refs):
-    shards, (*outs, panel, acc) = refs[:n_shards], refs[n_shards:]
-    slots, tile = tiles.shape[:2]
+            at = i * unroll + j
+            work(start + at, held, at)
+
+
+def forward_kernel(n_shards, count_ref, rows_ref, cols_ref, held, tiles, *refs):
+    shards, (rest, *outs, panel, acc, sems) = refs[:n_shards], refs[n_shards:]
+    start, tile = held.shape[:2]
     own = shards[0].shape[0]
     dump = acc.shape[0] - 1
     live = count_ref[0, 0]
     row, col = lax.axis_index("row"), lax.axis_index("col")
     line, core = col // CORES, col % CORES
 
+    copy, needed = tile_copies(tiles, start, rest.shape[0], live)
+
+    @pl.loop(0, needed)
+    def _(i):
+        copy(rest, sems, i).start()
+
     acc[...] = jnp.zeros_like(acc)
     for k in range(n_shards):
         panel[pl.ds(pl.multiple_of((row ^ k) * own, own), own), :] = shards[k][...]
 
-    def work(s):
+    def work(s, block, at):
         c = cols_ref[0, 0, s]
         r = jnp.where(s < live, rows_ref[0, 0, s], dump)
         source = panel[pl.ds(pl.multiple_of(c * tile, tile), tile), :]
-        acc[r] += jnp.dot(tiles[s], source, preferred_element_type=F32)
-
-    for_slots(live, slots, work)
+        acc[r] += jnp.dot(block[at], source, preferred_element_type=F32)
+
+    for_slots(live, held, 0, work)
+
+    @pl.loop(0, needed)
+    def _(i):
+        copy(rest, sems, i).wait()
+
+    for_slots(live, rest, start, work)
     per = own // tile
     half = outs[0].shape[0] // own
     for k in range(2 * half):
@@ -94,10 +115,10 @@
             outs[2 + spot(k, 2 * half)][span, :] = acc[(base + 1 - core) * per + b].astype(BF16)
 
 
-def backward_kernel(n_rows, n_lines, count_ref, rows_ref, cols_ref, tiles, *refs):
+def backward_kernel(n_rows, n_lines, count_ref, rows_ref, cols_ref, held, rest, *refs):
     n_cots = n_lines * CORES
     cots, outs, (turned, acc) = refs[:n_cots], refs[n_cots:-2], refs[-2:]
-    slots, tile = tiles.shape[:2]
+    start, tile = held.shape[:2]
     own = cots[0].shape[0]
     per = own // tile
     dump = acc.shape[0] - 1
@@ -111,15 +132,16 @@
         for b in range(per):
             turned[place + b] = cots[k][b * tile : (b + 1) * tile, :].T
 
-    def work(s):
+    def work(s, block, at):
         r = rows_ref[0, 0, s]
         c = jnp.where(s < live, cols_ref[0, 0, s], dump)
-        acc[c] += jnp.dot(turned[r], tiles[s], preferred_element_type=F32)
-
-    for_slots(live, slots, work)
+        acc[c] += jnp.dot(turned[r], block[at], preferred_element_type=F32)
+
+    for_slots(live, held, 0, work)
+    for_slots(live, rest, start, work)
     for k in range(n_rows):
         for b in range(per):
-            outs[k][b * tile : (b + 1) * tile, :] = acc[(row ^ k) * per + b].T.astype(BF16)
+            outs[k][b * tile : (b + 1) * tile, :] = acc[(row ^ k) * per + b].astype(BF16).T
 
 
 def weight_kernel(scale, stay, away, *refs):
@@ -188,31 +210,33 @@
     hidden = features[0] * relu_mask[0].astype(BF16)
     hids = [hidden] + [swap(hidden, "row", k) for k in range(1, n_rows)]
 
+    part = jax.ShapeDtypeStruct((slots // 2, tile, tile), BF16)
     held = pl.pallas_call(
         load_kernel,
-        out_shape=jax.ShapeDtypeStruct((slots, tile, tile), BF16),
+        out_shape=part,
         in_specs=[SMEM, ANY],
         out_specs=VMEM,
-        scratch_shapes=[pltpu.SemaphoreType.DMA((slots // math.gcd(slots, 8),))],
+        scratch_shapes=[pltpu.SemaphoreType.DMA((slots // 2 // math.gcd(slots // 2, 4),))],
         compiler_params=room(WORK),
         cost_estimate=cost(0, 2 * tiles.size),
         name="load_tiles",
     )(tile_count, tiles)
 
     half = jax.ShapeDtypeStruct((n_lines * own // 2, width), BF16)
-    keep_stay, keep_away, *send = pl.pallas_call(
+    rest, keep_stay, keep_away, *send = pl.pallas_call(
         functools.partial(forward_kernel, n_rows),
-        out_shape=(half,) * 2 + (block,) * n_lines,
-        in_specs=[SMEM] * 3 + [VMEM] * (1 + n_rows),
-        out_specs=(VMEM,) * (2 + n_lines),
+        out_shape=(part,) + (half,) * 2 + (block,) * n_lines,
+        in_specs=[SMEM] * 3 + [VMEM, ANY] + [VMEM] * n_rows,
+        out_specs=(VMEM,) * (3 + n_lines),
         scratch_shapes=[
             pltpu.VMEM((n_rows * own, width), BF16),
             pltpu.VMEM((row_blocks + 1, tile, width), F32),
+            pltpu.SemaphoreType.DMA((slots // 2 // math.gcd(slots // 2, 4),)),
         ],
         compiler_params=room(WORK),
         cost_estimate=cost(work, 2 * tiles.size),
         name="forward_tiles",
-    )(*ids, held, *hids)
+    )(*ids, held, tiles, *hids)
 
     def merge(keep, got):
         return pl.pallas_call(
@@ -253,7 +277,7 @@
     backs = pl.pallas_call(
         functools.partial(backward_kernel, n_rows, n_lines),
         out_shape=(block,) * n_rows,
-        in_specs=[SMEM] * 3 + [VMEM] * (1 + n_cols),
+        in_specs=[SMEM] * 3 + [VMEM] * (2 + n_cols),
         out_specs=(VMEM,) * n_rows,
         scratch_shapes=[
             pltpu.VMEM((row_blocks, width, tile), BF16),
@@ -262,7 +286,7 @@
         compiler_params=room(WORK),
         cost_estimate=cost(work, 2 * tiles.size),
         name="backward_tiles",
-    )(*ids, held, *cots)
+    )(*ids, held, rest, *cots)
     weight_term = weight_term + swap(weight_term, "col", 1)
     terms = [weight_term] + [swap(weight_term, "row", k) for k in range(1, n_rows)]
     backs, terms, got = lax.optimization_barrier((backs, terms, got))

time: 65.9 us -> 65.4 us (level)
  Pallas kernels: 25.8 us -> 22.2 us
  waiting for transfers between devices: 14.2 us -> 17.8 us
    ppermute x25, waiting for transfers between devices: 14.2 us -> 17.8 us  [swap(): return lax.ppermute(value, axis, [(i, i ^ step) for i in range(size)])]
    pallas_call x2, Pallas kernels: 16.9 us -> 13.5 us  [the longest x1 8.77 us: body(): pl.pallas_call(functools.partial(forward_kernel, n_rows), out_shape=(part...]
  transfers between devices with their start and end apart: 25 -> 25, of which waited for: 8 -> 10; matrix products, arithmetic and copies ran while one was open for 0% -> 0% of each run, Pallas kernels for 38% -> 32%
where the time goes in v4:
time: 65.4 us; the launch traced here: 65.3 us
  starting transfers between devices  22.5 us (34%)
  Pallas kernels  22.2 us (34%)
  waiting for transfers between devices  17.8 us (27%)
  between operations  1.49 us (2%)
  other arithmetic  1.2 us (2%)
    ppermute x25, starting transfers between devices, swap(): return lax.ppermute(value, axis, [(i, i ^ step) for i in range(size)])  22.5 us
    ppermute x25, waiting for transfers between devices, swap(): return lax.ppermute(value, axis, [(i, i ^ step) for i in range(size)])  17.8 us
    pallas_call x1, Pallas kernels, body(): pl.pallas_call(functools.partial(forward_kernel, n_rows), out_shape=(part...  8.77 us
    pallas_call x1, Pallas kernels, body(): pl.pallas_call(functools.partial(backward_kernel, n_rows, n_lines), out_s...  6.77 us
    pallas_call x1, Pallas kernels, body(): pl.pallas_call(load_kernel, out_shape=part, in_specs=[SMEM, ANY], out_spe...  4.69 us
  transfers between devices with their start and end apart: 25, of which 10 were waited for; matrix products, arithmetic and copies ran while one was open for 0% of the time, Pallas kernels for 32%

profile of v4, /device:TPU:0, one launch (start us, length us, event | category | flops | bytes accessed | tf_op | source)
XLA Modules:
  0.0 65.3 jit_solution(8465592297997960429)
XLA Ops:
  0.6 1.2 %multiply_bitcast_fusion.refs_0_ = bf16[1024,128]{1,0:T(8,128)(2,1)S(1)} fusion(bf16[1,1024,128]{2,1,0:T(8,128)(2,1)} %param.8, s32[1,1024,128]{2,1,0:T(8,128)} %mask.1), kind=kLoop, calls=%fused_computation | loop fusion | flops 262144 | bytes 1048576 | tf_op jit(solution)/shard_map/mul | solution.py:210
  1.8 3.0 %collective-permute-start = (bf16[1024,128]{1,0:T(8,128)(2,1)S(1)}, bf16[1024,128]{1,0:T(8,128)(2,1)S(1)}, u32[]{:S(2)}, u32[]{:S(2)}) collective-permute-start(bf16[1024,128]{1,0:T(8,128)(2,1)S(1)} %multiply_bitcast_fusion.refs_0_), channel_id=1, source_target_pairs={{0,8},{8,0},{16,24},{24,16},{1,9},{9,1},{17,25},{25,17},{2,10},{10... | collective-permute-start | bytes 786440 | tf_op jit(solution)/shard_map/ppermute | solution.py:24
  4.8 1.5 %collective-permute-start.1 = (bf16[1024,128]{1,0:T(8,128)(2,1)S(1)}, bf16[1024,128]{1,0:T(8,128)(2,1)S(1)}, u32[]{:S(2)}, u32[]{:S(2)}) collective-permute-start(bf16[1024,128]{1,0:T(8,128)(2,1)S(1)} %multiply_bitcast_fusion.refs_0_), channel_id=1, source_target_pairs={{0,16},{8,24},{16,0},{24,8},{1,17},{9,25},{17,1},{25,9},{2,18},{10... | collective-permute-start | bytes 786440 | tf_op jit(solution)/shard_map/ppermute | solution.py:24
  6.3 4.1 %collective-permute-start.10 = (bf16[1024,128]{1,0:T(8,128)(2,1)}, bf16[1024,128]{1,0:T(8,128)(2,1)S(1)}, u32[]{:S(2)}, u32[]{:S(2)}) collective-permute-start(bf16[1024,128]{1,0:T(8,128)(2,1)} %bitcast.3), channel_id=1, source_target_pairs={{0,6},{1,7},{2,4},{3,5},{4,2},{5,3},{6,0},{7,1},{8,14},{9,15},{10,... | collective-permute-start | bytes 786440 | tf_op jit(solution)/shard_map/ppermute | solution.py:24
  11.1 4.7 %load_tiles.1.held = bf16[92,256,256]{2,1,0:T(8,128)(2,1)S(1)} custom-call(s32[1,1]{1,0:T(1,128)S(6)} %copy.11.count_ref, bf16[1,1,184,256,256]{4,3,2,1,0:T(8,128)(2,1)} %tiles.3), custom_call_target="tpu_custom_call" | custom-call | bytes 24117248 | tf_op jit(solution)/shard_map/load_tiles/pallas_call | solution.py:214
  15.9 2.3 %collective-permute-done.1.refs_2_ = bf16[1024,128]{1,0:T(8,128)(2,1)S(1)} collective-permute-done((bf16[1024,128]{1,0:T(8,128)(2,1)S(1)}, bf16[1024,128]{1,0:T(8,128)(2,1)S(1)}, u32[]{:S(2)}, u32[]{:S(2)}) %collective-permute-start.1) | collective-permute-done | bytes 262176 | tf_op jit(solution)/shard_map/ppermute | solution.py:24
  18.2 8.8 %forward_tiles.1 = (bf16[92,256,256]{2,1,0:T(8,128)(2,1)S(1)}, bf16[2048,128]{1,0:T(8,128)(2,1)S(1)}, bf16[2048,128]{1,0:T(8,128)(2,1)S(1)}, bf16[1024,128]{1,0:...) custom-call(s32[1,1]{1,0:T(1,128)S(6)} %copy.11.count_ref, ...), custom_call_target="tpu_custom_call" | custom-call | flops 3087007744 | bytes 24117248 | tf_op jit(solution)/shard_map/forward_tiles/pallas_call | solution.py:226
  27.1 0.5 collective-permute-start.13
  27.7 4.4 %collective-permute-done.8.refs_4_.refs_2_ = bf16[1024,128]{1,0:T(8,128)(2,1)S(1)} collective-permute-done((bf16[1024,128]{1,0:T(8,128)(2,1)S(1)}, bf16[1024,128]{1,0:T(8,128)(2,1)S(1)}, u32[]{:S(2)}, u32[]{:S(2)}) %collective-permute-start.8) | collective-permute-done | bytes 262176 | tf_op jit(solution)/shard_map/ppermute | solution.py:24
  32.1 0.5 collective-permute-start.11
  32.7 0.4 collective-permute-start.9
  33.3 0.3 collective-permute-done.4.refs_1_
  33.6 0.4 collective-permute-done.11.refs_7_
  34.0 0.4 collective-permute-done.7.refs_3_
  34.4 0.4 collective-permute-done.9.refs_5_
  34.9 0.5 weight_term.1
  35.4 0.2 collective-permute-start.14
  35.6 1.1 %collective-permute-done.14 = f32[128,128]{1,0:T(8,128)S(1)} collective-permute-done((f32[128,128]{1,0:T(8,128)S(1)}, f32[128,128]{1,0:T(8,128)S(1)}, u32[]{:S(2)}, u32[]{:S(2)}) %collective-permute-start.14) | collective-permute-done | bytes 65568 | tf_op jit(solution)/shard_map/ppermute | solution.py:24
  36.7 1.6 %collective-permute-start.15 = (f32[128,128]{1,0:T(8,128)S(1)}, f32[128,128]{1,0:T(8,128)S(1)}, u32[]{:S(2)}, u32[]{:S(2)}) collective-permute-start(f32[128,128]{1,0:T(8,128)S(1)} %add.15), channel_id=1, source_target_pairs={{0,8},{8,0},{16,24},{24,16},{1,9},{9,1},{17,25},{25,17},{2,10},{10... | collective-permute-start | bytes 196616 | tf_op jit(solution)/shard_map/ppermute | solution.py:24
  38.2 1.5 %collective-permute-start.16 = (f32[128,128]{1,0:T(8,128)S(1)}, f32[128,128]{1,0:T(8,128)S(1)}, u32[]{:S(2)}, u32[]{:S(2)}) collective-permute-start(f32[128,128]{1,0:T(8,128)S(1)} %add.15), channel_id=1, source_target_pairs={{0,16},{8,24},{16,0},{24,8},{1,17},{9,25},{17,1},{25,9},{2,18},{10... | collective-permute-start | bytes 196616 | tf_op jit(solution)/shard_map/ppermute | solution.py:24
  39.8 0.5 collective-permute-start.17
  40.2 6.8 %backward_tiles.1 = (bf16[1024,128]{1,0:T(8,128)(2,1)S(1)}, bf16[1024,128]{1,0:T(8,128)(2,1)S(1)}, bf16[1024,128]{1,0:T(8,128)(2,1)S(1)}, bf16[1024,128]{1,0:T(8,128)(2,1)S(1)}) custom-call(s32[1,1]{1,0:T(1,128)S(6)} %copy.11.count_ref, s32[1,1,184]{2,1,0:T(1,128)S(1)} %copy-done.3, s32[1,1,184]{2,1,0:T(1,128)S(1)} %copy-done.4, ...), custom_call_target="tpu_custom_call" | custom-call | flops 3087007744 | bytes 24117248 | tf_op jit(solution)/shard_map/backward_tiles/pallas_call | solution.py:277
  47.1 0.2 collective-permute-done.18.right
  47.3 1.4 %collective-permute-start.19 = (bf16[1024,128]{1,0:T(8,128)(2,1)S(1)}, bf16[1024,128]{1,0:T(8,128)(2,1)S(1)}, u32[]{:S(2)}, u32[]{:S(2)}) collective-permute-start(bf16[1024,128]{1,0:T(8,128)(2,1)S(1)} %add_parts.3), channel_id=1, source_target_pairs={{0,4},{1,5},{2,6},{3,7},{4,0},{5,1},{6,2},{7,3},{8,12},{9,13},{10,... | collective-permute-start | bytes 786440 | tf_op jit(solution)/shard_map/ppermute | solution.py:24
  48.6 1.5 %collective-permute-start.20 = (bf16[1024,128]{1,0:T(8,128)(2,1)S(1)}, bf16[1024,128]{1,0:T(8,128)(2,1)S(1)}, u32[]{:S(2)}, u32[]{:S(2)}) collective-permute-start(bf16[1024,128]{1,0:T(8,128)(2,1)S(1)} %get-tuple-element.56), channel_id=1, source_target_pairs={{0,8},{8,0},{16,24},{24,16},{1,9},{9,1},{17,25},{25,17},{2,10},{10... | collective-permute-start | bytes 786440 | tf_op jit(solution)/shard_map/ppermute | solution.py:24
  50.1 1.5 %collective-permute-start.21 = (bf16[1024,128]{1,0:T(8,128)(2,1)S(1)}, bf16[1024,128]{1,0:T(8,128)(2,1)S(1)}, u32[]{:S(2)}, u32[]{:S(2)}) collective-permute-start(bf16[1024,128]{1,0:T(8,128)(2,1)S(1)} %get-tuple-element.57), channel_id=1, source_target_pairs={{0,16},{8,24},{16,0},{24,8},{1,17},{9,25},{17,1},{25,9},{2,18},{10... | collective-permute-start | bytes 786440 | tf_op jit(solution)/shard_map/ppermute | solution.py:24
  51.7 0.5 collective-permute-start.22
  52.1 1.8 %collective-permute-start.23 = (f32[128,128]{1,0:T(8,128)S(1)}, f32[128,128]{1,0:T(8,128)S(1)}, u32[]{:S(2)}, u32[]{:S(2)}) collective-permute-start(f32[128,128]{1,0:T(8,128)S(1)} %add_add_fusion), channel_id=1, source_target_pairs={{0,2},{1,3},{2,0},{3,1},{4,6},{5,7},{6,4},{7,5},{8,10},{9,11},{10,... | collective-permute-start | bytes 196616 | tf_op jit(solution)/shard_map/ppermute | solution.py:24
  54.0 2.5 %collective-permute-done.23 = f32[128,128]{1,0:T(8,128)S(1)} collective-permute-done((f32[128,128]{1,0:T(8,128)S(1)}, f32[128,128]{1,0:T(8,128)S(1)}, u32[]{:S(2)}, u32[]{:S(2)}) %collective-permute-start.23) | collective-permute-done | bytes 65568 | tf_op jit(solution)/shard_map/ppermute | solution.py:24
  56.5 1.7 %collective-permute-start.24 = (f32[128,128]{1,0:T(8,128)S(1)}, f32[128,128]{1,0:T(8,128)S(1)}, u32[]{:S(2)}, u32[]{:S(2)}) collective-permute-start(f32[128,128]{1,0:T(8,128)S(1)} %add.19.refs_4_), channel_id=1, source_target_pairs={{0,4},{1,5},{2,6},{3,7},{4,0},{5,1},{6,2},{7,3},{8,12},{9,13},{10,... | collective-permute-start | bytes 196616 | tf_op jit(solution)/shard_map/ppermute | solution.py:24
  58.3 5.9 %collective-permute-done.24.refs_5_ = f32[128,128]{1,0:T(8,128)S(1)} collective-permute-done((f32[128,128]{1,0:T(8,128)S(1)}, f32[128,128]{1,0:T(8,128)S(1)}, u32[]{:S(2)}, u32[]{:S(2)}) %collective-permute-start.24) | collective-permute-done | bytes 65568 | tf_op jit(solution)/shard_map/ppermute | solution.py:24
  64.1 1.1 %finish.1 = (bf16[1,1024,128]{2,1,0:T(8,128)(2,1)}, f32[128,128]{1,0:T(8,128)}, bf16[1,1024,128]{2,1,0:T(8,128)(2,1)}) custom-call(bf16[128,128]{1,0:T(8,128)(2,1)S(1)} %copy-done.2, s32[1,1024,128]{2,1,0:T(8,128)S(1)} %copy-done, bf16[1024,128]{1,0:T(8,128)(2,1)S(1)} %add_parts.2.stay, bf16[1024,128]{1,0:T(8,128)(2,1)S(1)} %collective-permute-done.19.got, ...), custom_call_target="tpu_custom_call" | custom-call | tf_op jit(solution)/shard_map/finish/pallas_call | solution.py:304
  (41 shorter events, 0.9 us)
Async XLA Ops:
  1.8 14.0 %collective-permute-start = (bf16[1024,128]{1,0:T(8,128)(2,1)S(1)}, bf16[1024,128]{1,0:T(8,128)(2,1)S(1)}, u32[]{:S(2)}, u32[]{:S(2)}) collective-permute-start(bf16[1024,128]{1,0:T(8,128)(2,1)S(1)} %multiply_bitcast_fusion.refs_0_), channel_id=1, source_target_pairs={{0,8},{8,0},{16,24},{24,16},{1,9},{9,1},{17,25},{25,17},{2,10},{10... | collective-permute-start | bytes 786440 | tf_op jit(solution)/shard_map/ppermute | solution.py:24
  4.8 13.4 %collective-permute-start.1 = (bf16[1024,128]{1,0:T(8,128)(2,1)S(1)}, bf16[1024,128]{1,0:T(8,128)(2,1)S(1)}, u32[]{:S(2)}, u32[]{:S(2)}) collective-permute-start(bf16[1024,128]{1,0:T(8,128)(2,1)S(1)} %multiply_bitcast_fusion.refs_0_), channel_id=1, source_target_pairs={{0,16},{8,24},{16,0},{24,8},{1,17},{9,25},{17,1},{25,9},{2,18},{10... | collective-permute-start | bytes 786440 | tf_op jit(solution)/shard_map/ppermute | solution.py:24
  6.3 11.9 %collective-permute-start.2 = (bf16[1024,128]{1,0:T(8,128)(2,1)S(1)}, bf16[1024,128]{1,0:T(8,128)(2,1)S(1)}, u32[]{:S(2)}, u32[]{:S(2)}) collective-permute-start(bf16[1024,128]{1,0:T(8,128)(2,1)S(1)} %multiply_bitcast_fusion.refs_0_), channel_id=1, source_target_pairs={{0,24},{8,16},{16,8},{24,0},{1,25},{9,17},{17,9},{25,1},{2,26},{10... | collective-permute-start | bytes 786440 | tf_op jit(solution)/shard_map/ppermute | solution.py:24
  6.3 20.7 %collective-permute-start.10 = (bf16[1024,128]{1,0:T(8,128)(2,1)}, bf16[1024,128]{1,0:T(8,128)(2,1)S(1)}, u32[]{:S(2)}, u32[]{:S(2)}) collective-permute-start(bf16[1024,128]{1,0:T(8,128)(2,1)} %bitcast.3), channel_id=1, source_target_pairs={{0,6},{1,7},{2,4},{3,5},{4,2},{5,3},{6,0},{7,1},{8,14},{9,15},{10,... | collective-permute-start | bytes 786440 | tf_op jit(solution)/shard_map/ppermute | solution.py:24
  10.4 17.2 %collective-permute-start.6 = (bf16[1024,128]{1,0:T(8,128)(2,1)}, bf16[1024,128]{1,0:T(8,128)(2,1)S(1)}, u32[]{:S(2)}, u32[]{:S(2)}) collective-permute-start(bf16[1024,128]{1,0:T(8,128)(2,1)} %bitcast.4), channel_id=1, source_target_pairs={{0,2},{1,3},{2,0},{3,1},{4,6},{5,7},{6,4},{7,5},{8,10},{9,11},{10,... | collective-permute-start | bytes 786440 | tf_op jit(solution)/shard_map/ppermute | solution.py:24
  11.1 4.7 %copy-start.1 = (bf16[1,1024,128]{2,1,0:T(8,128)(2,1)S(1)}, bf16[1,1024,128]{2,1,0:T(8,128)(2,1)}, u32[]{:S(2)}) copy-start(bf16[1,1024,128]{2,1,0:T(8,128)(2,1)} %param.15) | copy-start | bytes 786436
  11.1 7.1 %copy-start.3 = (s32[1,1,184]{2,1,0:T(1,128)S(1)}, s32[1,1,184]{2,1,0:T(1,128)}, u32[]{:S(2)}) copy-start(s32[1,1,184]{2,1,0:T(1,128)} %rows_ref.3) | copy-start | bytes 2212
  11.1 7.1 %copy-start.4 = (s32[1,1,184]{2,1,0:T(1,128)S(1)}, s32[1,1,184]{2,1,0:T(1,128)}, u32[]{:S(2)}) copy-start(s32[1,1,184]{2,1,0:T(1,128)} %cols_ref.3) | copy-start | bytes 2212
  15.8 16.3 %collective-permute-start.8 = (bf16[1024,128]{1,0:T(8,128)(2,1)S(1)}, bf16[1024,128]{1,0:T(8,128)(2,1)S(1)}, u32[]{:S(2)}, u32[]{:S(2)}) collective-permute-start(bf16[1024,128]{1,0:T(8,128)(2,1)S(1)} %bitcast.5), channel_id=1, source_target_pairs={{0,4},{1,5},{2,6},{3,7},{4,0},{5,1},{6,2},{7,3},{8,12},{9,13},{10,... | collective-permute-start | bytes 786440 | tf_op jit(solution)/shard_map/ppermute | solution.py:24
  18.2 13.9 %collective-permute-start.5 = (bf16[1024,128]{1,0:T(8,128)(2,1)S(1)}, bf16[1024,128]{1,0:T(8,128)(2,1)S(1)}, u32[]{:S(2)}, u32[]{:S(2)}) collective-permute-start(bf16[1024,128]{1,0:T(8,128)(2,1)S(1)} %bitcast.6), channel_id=1, source_target_pairs={{0,1},{1,0},{2,3},{3,2},{4,5},{5,4},{6,7},{7,6},{8,9},{9,8},{10,11... | collective-permute-start | bytes 786440 | tf_op jit(solution)/shard_map/ppermute | solution.py:24
  27.0 5.6 %collective-permute-start.12 = (bf16[1024,128]{1,0:T(8,128)(2,1)S(1)}, bf16[1024,128]{1,0:T(8,128)(2,1)S(1)}, u32[]{:S(2)}, u32[]{:S(2)}) collective-permute-start(bf16[1024,128]{1,0:T(8,128)(2,1)S(1)} %get-tuple-element.52), channel_id=1, source_target_pairs={{0,1},{1,0},{2,3},{3,2},{4,5},{5,4},{6,7},{7,6},{8,9},{9,8},{10,11... | collective-permute-start | bytes 786440 | tf_op jit(solution)/shard_map/ppermute | solution.py:24
  27.1 5.6 %collective-permute-start.13 = (bf16[1024,128]{1,0:T(8,128)(2,1)S(1)}, bf16[1024,128]{1,0:T(8,128)(2,1)S(1)}, u32[]{:S(2)}, u32[]{:S(2)}) collective-permute-start(bf16[1024,128]{1,0:T(8,128)(2,1)S(1)} %get-tuple-element.53), channel_id=1, source_target_pairs={{0,1},{1,0},{2,3},{3,2},{4,5},{5,4},{6,7},{7,6},{8,9},{9,8},{10,11... | collective-permute-start | bytes 786440 | tf_op jit(solution)/shard_map/ppermute | solution.py:24
  27.6 5.7 %collective-permute-start.3 = (bf16[1024,128]{1,0:T(8,128)(2,1)S(1)}, bf16[1024,128]{1,0:T(8,128)(2,1)S(1)}, u32[]{:S(2)}, u32[]{:S(2)}) collective-permute-start(bf16[1024,128]{1,0:T(8,128)(2,1)S(1)} %get-tuple-element.34), channel_id=1, source_target_pairs={{0,1},{1,0},{2,3},{3,2},{4,5},{5,4},{6,7},{7,6},{8,9},{9,8},{10,11... | collective-permute-start | bytes 786440 | tf_op jit(solution)/shard_map/ppermute | solution.py:24
  32.1 1.5 %collective-permute-start.4 = (bf16[1024,128]{1,0:T(8,128)(2,1)S(1)}, bf16[1024,128]{1,0:T(8,128)(2,1)S(1)}, u32[]{:S(2)}, u32[]{:S(2)}) collective-permute-start(bf16[1024,128]{1,0:T(8,128)(2,1)S(1)} %get-tuple-element.35), channel_id=1, source_target_pairs={{0,1},{1,0},{2,3},{3,2},{4,5},{5,4},{6,7},{7,6},{8,9},{9,8},{10,11... | collective-permute-start | bytes 786440 | tf_op jit(solution)/shard_map/ppermute | solution.py:24
  32.1 1.9 %collective-permute-start.11 = (bf16[1024,128]{1,0:T(8,128)(2,1)S(1)}, bf16[1024,128]{1,0:T(8,128)(2,1)S(1)}, u32[]{:S(2)}, u32[]{:S(2)}) collective-permute-start(bf16[1024,128]{1,0:T(8,128)(2,1)S(1)} %collective-permute-done.10.refs_6_.refs_3_), channel_id=1, source_target_pairs={{0,1},{1,0},{2,3},{3,2},{4,5},{5,4},{6,7},{7,6},{8,9},{9,8},{10,11... | collective-permute-start | bytes 786440 | tf_op jit(solution)/shard_map/ppermute | solution.py:24
  32.6 1.8 %collective-permute-start.7 = (bf16[1024,128]{1,0:T(8,128)(2,1)S(1)}, bf16[1024,128]{1,0:T(8,128)(2,1)S(1)}, u32[]{:S(2)}, u32[]{:S(2)}) collective-permute-start(bf16[1024,128]{1,0:T(8,128)(2,1)S(1)} %collective-permute-done.6.refs_2_.refs_1_), channel_id=1, source_target_pairs={{0,1},{1,0},{2,3},{3,2},{4,5},{5,4},{6,7},{7,6},{8,9},{9,8},{10,11... | collective-permute-start | bytes 786440 | tf_op jit(solution)/shard_map/ppermute | solution.py:24
  32.7 2.1 %collective-permute-start.9 = (bf16[1024,128]{1,0:T(8,128)(2,1)S(1)}, bf16[1024,128]{1,0:T(8,128)(2,1)S(1)}, u32[]{:S(2)}, u32[]{:S(2)}) collective-permute-start(bf16[1024,128]{1,0:T(8,128)(2,1)S(1)} %collective-permute-done.8.refs_4_.refs_2_), channel_id=1, source_target_pairs={{0,1},{1,0},{2,3},{3,2},{4,5},{5,4},{6,7},{7,6},{8,9},{9,8},{10,11... | collective-permute-start | bytes 786440 | tf_op jit(solution)/shard_map/ppermute | solution.py:24
  33.2 14.0 %collective-permute-start.18 = (bf16[2048,128]{1,0:T(8,128)(2,1)S(1)}, bf16[2048,128]{1,0:T(8,128)(2,1)S(1)}, u32[]{:S(2)}, u32[]{:S(2)}) collective-permute-start(bf16[2048,128]{1,0:T(8,128)(2,1)S(1)} %merge_parts.3.away), channel_id=1, source_target_pairs={{0,2},{1,3},{2,0},{3,1},{4,6},{5,7},{6,4},{7,5},{8,10},{9,11},{10,... | collective-permute-start | bytes 1572872 | tf_op jit(solution)/shard_map/ppermute | solution.py:24
  35.4 1.3 %collective-permute-start.14 = (f32[128,128]{1,0:T(8,128)S(1)}, f32[128,128]{1,0:T(8,128)S(1)}, u32[]{:S(2)}, u32[]{:S(2)}) collective-permute-start(f32[128,128]{1,0:T(8,128)S(1)} %weight_term.1), channel_id=1, source_target_pairs={{0,1},{1,0},{2,3},{3,2},{4,5},{5,4},{6,7},{7,6},{8,9},{9,8},{10,11... | collective-permute-start | bytes 196616 | tf_op jit(solution)/shard_map/ppermute | solution.py:24
  36.7 10.3 %collective-permute-start.15 = (f32[128,128]{1,0:T(8,128)S(1)}, f32[128,128]{1,0:T(8,128)S(1)}, u32[]{:S(2)}, u32[]{:S(2)}) collective-permute-start(f32[128,128]{1,0:T(8,128)S(1)} %add.15), channel_id=1, source_target_pairs={{0,8},{8,0},{16,24},{24,16},{1,9},{9,1},{17,25},{25,17},{2,10},{10... | collective-permute-start | bytes 196616 | tf_op jit(solution)/shard_map/ppermute | solution.py:24
  38.2 8.8 %collective-permute-start.16 = (f32[128,128]{1,0:T(8,128)S(1)}, f32[128,128]{1,0:T(8,128)S(1)}, u32[]{:S(2)}, u32[]{:S(2)}) collective-permute-start(f32[128,128]{1,0:T(8,128)S(1)} %add.15), channel_id=1, source_target_pairs={{0,16},{8,24},{16,0},{24,8},{1,17},{9,25},{17,1},{25,9},{2,18},{10... | collective-permute-start | bytes 196616 | tf_op jit(solution)/shard_map/ppermute | solution.py:24
  39.8 7.3 %collective-permute-start.17 = (f32[128,128]{1,0:T(8,128)S(1)}, f32[128,128]{1,0:T(8,128)S(1)}, u32[]{:S(2)}, u32[]{:S(2)}) collective-permute-start(f32[128,128]{1,0:T(8,128)S(1)} %add.15), channel_id=1, source_target_pairs={{0,24},{8,16},{16,8},{24,0},{1,25},{9,17},{17,9},{25,1},{2,26},{10... | collective-permute-start | bytes 196616 | tf_op jit(solution)/shard_map/ppermute | solution.py:24
  40.2 23.9 %copy-start = (s32[1,1024,128]{2,1,0:T(8,128)S(1)}, s32[1,1024,128]{2,1,0:T(8,128)}, u32[]{:S(2)}) copy-start(s32[1,1024,128]{2,1,0:T(8,128)} %mask.1) | copy-start | bytes 1572868
  40.2 23.9 %copy-start.2 = (bf16[128,128]{1,0:T(8,128)(2,1)S(1)}, bf16[128,128]{1,0:T(8,128)(2,1)}, u32[]{:S(2)}) copy-start(bf16[128,128]{1,0:T(8,128)(2,1)} %weight.1) | copy-start | bytes 98308
  47.3 16.8 %collective-permute-start.19 = (bf16[1024,128]{1,0:T(8,128)(2,1)S(1)}, bf16[1024,128]{1,0:T(8,128)(2,1)S(1)}, u32[]{:S(2)}, u32[]{:S(2)}) collective-permute-start(bf16[1024,128]{1,0:T(8,128)(2,1)S(1)} %add_parts.3), channel_id=1, source_target_pairs={{0,4},{1,5},{2,6},{3,7},{4,0},{5,1},{6,2},{7,3},{8,12},{9,13},{10,... | collective-permute-start | bytes 786440 | tf_op jit(solution)/shard_map/ppermute | solution.py:24
  48.6 15.5 %collective-permute-start.20 = (bf16[1024,128]{1,0:T(8,128)(2,1)S(1)}, bf16[1024,128]{1,0:T(8,128)(2,1)S(1)}, u32[]{:S(2)}, u32[]{:S(2)}) collective-permute-start(bf16[1024,128]{1,0:T(8,128)(2,1)S(1)} %get-tuple-element.56), channel_id=1, source_target_pairs={{0,8},{8,0},{16,24},{24,16},{1,9},{9,1},{17,25},{25,17},{2,10},{10... | collective-permute-start | bytes 786440 | tf_op jit(solution)/shard_map/ppermute | solution.py:24
  50.1 14.0 %collective-permute-start.21 = (bf16[1024,128]{1,0:T(8,128)(2,1)S(1)}, bf16[1024,128]{1,0:T(8,128)(2,1)S(1)}, u32[]{:S(2)}, u32[]{:S(2)}) collective-permute-start(bf16[1024,128]{1,0:T(8,128)(2,1)S(1)} %get-tuple-element.57), channel_id=1, source_target_pairs={{0,16},{8,24},{16,0},{24,8},{1,17},{9,25},{17,1},{25,9},{2,18},{10... | collective-permute-start | bytes 786440 | tf_op jit(solution)/shard_map/ppermute | solution.py:24
  51.7 12.5 %collective-permute-start.22 = (bf16[1024,128]{1,0:T(8,128)(2,1)S(1)}, bf16[1024,128]{1,0:T(8,128)(2,1)S(1)}, u32[]{:S(2)}, u32[]{:S(2)}) collective-permute-start(bf16[1024,128]{1,0:T(8,128)(2,1)S(1)} %get-tuple-element.58), channel_id=1, source_target_pairs={{0,24},{8,16},{16,8},{24,0},{1,25},{9,17},{17,9},{25,1},{2,26},{10... | collective-permute-start | bytes 786440 | tf_op jit(solution)/shard_map/ppermute | solution.py:24
  52.1 4.3 %collective-permute-start.23 = (f32[128,128]{1,0:T(8,128)S(1)}, f32[128,128]{1,0:T(8,128)S(1)}, u32[]{:S(2)}, u32[]{:S(2)}) collective-permute-start(f32[128,128]{1,0:T(8,128)S(1)} %add_add_fusion), channel_id=1, source_target_pairs={{0,2},{1,3},{2,0},{3,1},{4,6},{5,7},{6,4},{7,5},{8,10},{9,11},{10,... | collective-permute-start | bytes 196616 | tf_op jit(solution)/shard_map/ppermute | solution.py:24
  56.5 7.6 %collective-permute-start.24 = (f32[128,128]{1,0:T(8,128)S(1)}, f32[128,128]{1,0:T(8,128)S(1)}, u32[]{:S(2)}, u32[]{:S(2)}) collective-permute-start(f32[128,128]{1,0:T(8,128)S(1)} %add.19.refs_4_), channel_id=1, source_target_pairs={{0,4},{1,5},{2,6},{3,7},{4,0},{5,1},{6,2},{7,3},{8,12},{9,13},{10,... | collective-permute-start | bytes 196616 | tf_op jit(solution)/shard_map/ppermute | solution.py:24
